TPU v7x, 32 devices: a whole 2x2x4 slice. The times are simulated.
32 devices in a mesh: inner: 16 (over z, y, x), outer: 2 (over core).
Axes of the slice: x: 2, y: 2, z: 4, core: 2. Of those that a mesh axis runs over, the one named last changes fastest.
Arguments:
- feats_first: bfloat16 [2, 4096, 2048], P('outer', 'inner'), may hold values from -4 to 8
- feats_second: bfloat16 [2, 4096, 2048], P('outer', 'inner'), may hold values from -4 to 8
- expander: bfloat16 [2048, 1024], P('inner'), may hold values from -0.125 to 0.125
- tile_count: int32 [2, 16], replicated, may hold values from 64 to 256, as said below
- match_dev: int32 [2, 4096, 1], P('outer', 'inner'), may hold values from 0 to 15; in each aligned block of 256 rows (0 to 255, 256 to 511, ..., all dimensions but the last counted through in order) at most 48 rows name the same one
- match_tile: int32 [2, 4096], P('outer', 'inner'), may hold values from 0 to 255
Outputs:
- covariance: float32 [1024, 1024], P('inner')
- invariance: float32 [2, 4096], P('outer', 'inner')
Inputs may be any that keep to these rules, and one draw needn't show every extreme that they name: `tile_count`: for every slide some device has all 256 tiles live; the others at least a quarter. `match_dev`: at most 48 tiles of one device name the same device.
All inputs are finite; a program needn't handle non-finite values.
Results may differ from a plain program's by a relative error of at most 0.00135.
Values may be sent and summed in bfloat16 or wider, within the bound.
A program may use at most 64 MiB of HBM per device.

v0:
```python
import jax
import jax.numpy as jnp
from jax import lax
from jax.sharding import PartitionSpec as P


def shards(feats_first, feats_second, expander, tile_count, match_dev, match_tile):
    first_rows = feats_first[0]
    second_rows = feats_second[0]
    tile_rows = first_rows.shape[0]
    expand_width = expander.shape[1]
    group_size = lax.axis_size("inner")
    capacity = max(2, 3 * tile_rows // group_size)
    inner_pos = lax.axis_index("inner")
    outer_pos = lax.axis_index("outer")
    piece = lax.all_gather(expander, "inner", axis=0, tiled=True)
    first_acc = jnp.dot(first_rows, piece, preferred_element_type=jnp.float32)
    second_acc = jnp.dot(second_rows, piece, preferred_element_type=jnp.float32)
    first_embed = first_acc.astype(jnp.bfloat16)
    second_embed = second_acc.astype(jnp.bfloat16)
    counts = lax.dynamic_index_in_dim(tile_count, outer_pos, 0, keepdims=False)
    own_count = lax.dynamic_index_in_dim(counts, inner_pos, 0, keepdims=False)
    row_index = jnp.arange(tile_rows, dtype=jnp.int32)
    live = row_index < own_count
    target_dev = match_dev[0, :, 0]
    target_tile = match_tile[0]
    onehot = (target_dev[:, None] == jnp.arange(group_size, dtype=jnp.int32)[None, :]).astype(
        jnp.int32
    )
    slot_pos = jnp.sum((jnp.cumsum(onehot, axis=0) - 1) * onehot, axis=1)
    send_rows = (
        jnp.zeros((group_size, capacity, expand_width), jnp.bfloat16)
        .at[target_dev, slot_pos]
        .set(first_embed)
    )
    send_tiles = (
        jnp.zeros((group_size, capacity), jnp.int32).at[target_dev, slot_pos].set(target_tile)
    )
    recv_rows, recv_tiles = (
        lax.all_to_all(send_rows, "inner", split_axis=0, concat_axis=0, tiled=True),
        lax.all_to_all(send_tiles, "inner", split_axis=0, concat_axis=0, tiled=True),
    )
    partner = second_embed[recv_tiles]
    diff = recv_rows.astype(jnp.float32) - partner.astype(jnp.float32)
    distance = jnp.where(recv_tiles < own_count, jnp.mean(diff * diff, axis=-1), jnp.float32(0.0))
    returned = lax.all_to_all(distance, "inner", split_axis=0, concat_axis=0, tiled=True)
    dest_count = counts[target_dev]
    valid = live & (target_tile < dest_count)
    invariance = jnp.where(valid, returned[target_dev, slot_pos], jnp.float32(0.0))
    masked = jnp.where(live[:, None], first_embed, jnp.zeros_like(first_embed))
    column_total = lax.psum(jnp.sum(masked.astype(jnp.float32), axis=0), ("inner", "outer"))
    total = jnp.sum(tile_count).astype(jnp.float32)
    share_rows = expand_width // group_size
    local_share = lax.psum_scatter(
        lax.dot_general(
            masked, masked, (((0,), (0,)), ((), ())), preferred_element_type=jnp.float32
        ),
        "inner",
        scatter_dimension=0,
        tiled=True,
    )
    gram_share = lax.psum(local_share, "outer")
    own_sums = lax.dynamic_slice_in_dim(column_total, inner_pos * share_rows, share_rows, 0)
    covariance = (gram_share - own_sums[:, None] * column_total[None, :] / total) / (total - 1.0)
    return (covariance, invariance[None, :])


def solution(mesh):
    return jax.shard_map(
        shards,
        mesh=mesh,
        in_specs=(
            P("outer", "inner", None),
            P("outer", "inner", None),
            P("inner", None),
            P(),
            P("outer", "inner", None),
            P("outer", "inner"),
        ),
        out_specs=(P("inner", None), P("outer", "inner")),
        check_vma=False,
    )
```

profile of v0, /device:TPU:13, one launch (start us, length us, event | category | flops | bytes accessed | tf_op | source)
XLA Modules:
  0.0 290.7 jit_solution(2286077928159644080)
XLA Ops:
  7.2 0.0 copy-start
  7.2 0.0 all-gather.2.cloned.1.call-start
  7.2 0.7 all-gather.2.cloned.1.call-update
  7.9 0.0 reduce-scatter.2.cloned.1.call-start
  8.0 1.3 dynamic_slice.11
  9.3 0.6 iota_compare_fusion.2
  10.0 76.9 %all-gather.2.cloned.1.call-done = bf16[2048,1024]{1,0:T(8,128)(2,1)} async-done(((bf16[128,1024]{1,0:T(8,128)(2,1)}), bf16[2048,1024]{1,0:T(8,128)(2,1)}) %all-gather.2.cloned.1.call-update) | async-done | bytes 4194320 | tf_op jit(solution)/shard_map/all_gather | solution.py:16
  86.9 0.0 copy-done
  86.9 3.4 %convert_reduce_fusion = (f32[1024]{0:T(1024)S(1)}, bf16[256,1024]{1,0:T(8,128)(2,1)S(1)}) fusion(pred[256]{0:T(512)(128)(4,1)S(1)} %iota_compare_fusion.2, bf16[2048,1024]{1,0:T(8,128)(2,1)} %all-gather.2.cloned.1.call-done, bf16[1,256,2048]{2,1,0:T(8,128)(2,1)S(1)} %copy-done), kind=kOutput, calls=%fused_computation.11 | convolution fusion | flops 1074789376 | bytes 5771520 | tf_op jit(solution)/shard_map/dot_general | solution.py:17
  90.3 2.8 fusion.4
  93.1 0.0 copy-start.1
  93.1 0.0 copy-start.3
  93.1 0.0 copy-start.2
  93.1 0.0 reduce-scatter.2.cloned.1.call-update
  93.1 0.6 copy-done.1
  93.8 0.6 reduce-window.6
  94.4 0.2 slice_reduce_fusion
  94.6 0.0 copy-done.3
  94.6 0.7 fusion.11
  95.3 0.1 fusion.6
  95.4 4.3 %compare_select_fusion.4 = (s32[256,1]{0,1:T(1,128)S(1)}, s32[256,1]{0,1:T(1,128)S(1)}) fusion(s32[]{:T(128)} %bitcast.12, s32[]{:T(128)} %bitcast.13, s32[]{:T(128)} %bitcast.14, s32[]{:T(128)} %bitcast.15, s32[]{:T(128)} %bitcast.16, s32[]{:T(128)} %bitcast.18, s32[]{:T(128)} %bitcast.17, s32[1,256,1]{1,2,0:T(1,128)S(1)} %copy-done.1), kind=kLoop, calls=%fused_computation.38 | loop fusion | flops 3840 | bytes 3100 | tf_op jit(solution)/shard_map/gather | solution.py:47
  99.7 0.6 broadcast.105
  100.3 0.0 copy-done.2
  100.3 36.3 %scatter_fusion = s32[16,48]{1,0:T(8,128)} fusion(s32[16,48]{1,0:T(8,128)} %broadcast.105, s32[256]{0:T(256)S(1)} %bitcast.67, s32[256]{0:T(256)S(1)} %bitcast.75), kind=kCustom, calls=%fused_computation.2 | custom fusion | bytes 5120 | tf_op jit(solution)/shard_map/scatter | solution.py:37
  136.6 5.2 %all-to-all-start = ((s32[16,1,48]{2,1,0:T(1,128)}), s32[16,1,48]{2,1,0:T(1,128)S(1)}, u32[]{:S(2)}, u32[]{:S(2)}) async-start(s32[16,1,48]{2,1,0:T(1,128)} %bitcast.28), calls=%async_computation.1 | async-start | bytes 16384 | tf_op jit(solution)/shard_map/all_to_all | solution.py:41
  141.8 1.4 broadcast_in_dim.22
  143.3 36.8 %scatter_fusion.1 = bf16[16,48,1024]{2,1,0:T(8,128)(2,1)} fusion(bf16[16,48,1024]{2,1,0:T(8,128)(2,1)} %broadcast_in_dim.22, s32[256]{0:T(256)S(1)} %bitcast.68, bf16[256,1024]{1,0:T(8,128)(2,1)S(1)} %get-tuple-element.32), kind=kCustom, calls=%fused_computation.3 | custom fusion | bytes 1574912 | tf_op jit(solution)/shard_map/scatter | solution.py:34
  180.1 0.0 all-to-all-done
  180.1 6.5 %all-to-all-start.1 = ((bf16[16,48,1024]{2,1,0:T(8,128)(2,1)}), bf16[16,48,1024]{2,1,0:T(8,128)(2,1)S(1)}, u32[]{:S(2)}, u32[]{:S(2)}) async-start(bf16[16,48,1024]{2,1,0:T(8,128)(2,1)} %scatter_fusion.1), calls=%async_computation.2 | async-start | bytes 3145728 | tf_op jit(solution)/shard_map/all_to_all | solution.py:40
  186.7 0.1 reshape.148
  186.7 3.8 %convolution_convert_fusion = bf16[256,1024]{1,0:T(8,128)(2,1)S(1)} fusion(bf16[2048,1024]{1,0:T(8,128)(2,1)} %all-gather.2.cloned.1.call-done, bf16[1,256,2048]{2,1,0:T(8,128)(2,1)} %param.7), kind=kOutput, calls=%fused_computation.7 | convolution fusion | flops 1074003968 | bytes 5767168 | tf_op jit(solution)/shard_map/dot_general | solution.py:18
  190.5 3.6 %gather_fusion = bf16[768,1024]{1,0:T(8,128)(2,1)} fusion(bf16[256,1024]{1,0:T(8,128)(2,1)S(1)} %convolution_convert_fusion, s32[1024]{0:T(1024)S(1)} %pad_clamp_fusion), kind=kCustom, calls=%fused_computation | custom fusion | bytes 3148800 | tf_op jit(solution)/shard_map/gather | solution.py:43
  194.1 29.5 %all-to-all-done.1 = bf16[16,48,1024]{2,1,0:T(8,128)(2,1)S(1)} async-done(((bf16[16,48,1024]{2,1,0:T(8,128)(2,1)}), bf16[16,48,1024]{2,1,0:T(8,128)(2,1)S(1)}, u32[]{:S(2)}, u32[]{:S(2)}) %all-to-all-start.1) | async-done | bytes 1572896 | tf_op jit(solution)/shard_map/all_to_all | solution.py:40
  223.6 2.0 fusion.1
  225.6 1.2 compare_select_fusion
  226.8 3.9 %all-to-all-start.2 = ((f32[16,1,48]{2,1,0:T(1,128)}), f32[16,1,48]{2,1,0:T(1,128)S(1)}, u32[]{:S(2)}, u32[]{:S(2)}) async-start(f32[16,1,48]{2,1,0:T(1,128)} %compare_select_fusion), calls=%async_computation.3 | async-start | bytes 16384 | tf_op jit(solution)/shard_map/all_to_all | solution.py:46
  230.8 0.0 all-reduce.2.cloned.1.call-start
  230.8 0.0 reduce-scatter.2.cloned.1.call-done
  230.9 0.7 all-reduce.2.cloned.1.call-update
  231.5 5.6 %select_select_fusion = s32[256]{0:T(256)S(1)} fusion(pred[256]{0:T(512)(128)(4,1)S(1)} %get-tuple-element.10, pred[256]{0:T(512)(128)(4,1)S(1)} %get-tuple-element.9, pred[256]{0:T(512)(128)(4,1)S(1)} %get-tuple-element.8, pred[256]{0:T(512)(128)(4,1)S(1)} %get-tuple-element.7, pred[256]{0:T(512)(128)(4,1)S(1)} %get-tuple-element.6, ...), kind=kLoop, calls=%fused_computation.49 | loop fusion | flops 2304 | bytes 4388 | tf_op jit(solution)/shard_map/gather | solution.py:47
  237.2 0.6 reduce_sum.39
  238.5 40.7 %psum.15 = f32[1024]{0:T(1024)S(1)} all-reduce(f32[1024]{0:T(1024)S(1)} %get-tuple-element.31), channel_id=1, replica_groups=mesh['inner'=16,'outer'=2] {'inner','outer'}, use_global_device_ids=true, to_apply=%region_3.4 | all-reduce | flops 1024 | bytes 8192 | tf_op jit(solution)/shard_map/psum | solution.py:51
  279.2 0.1 dynamic_slice.12
  279.2 0.0 all-to-all-done.2
  279.2 1.9 gather_fusion.1
  281.2 1.2 and_select_fusion
  282.4 0.0 all-reduce.2.cloned.1.call-done
  282.4 1.8 subtract_divide_fusion
  (9 shorter events, 0.1 us)
Async XLA Ops:
  7.2 79.7 %copy-start = (bf16[1,256,2048]{2,1,0:T(8,128)(2,1)S(1)}, bf16[1,256,2048]{2,1,0:T(8,128)(2,1)}, u32[]{:S(2)}) copy-start(bf16[1,256,2048]{2,1,0:T(8,128)(2,1)} %param.6) | copy-start | bytes 3145732
  7.2 79.7 %all-gather.2.cloned.1.call-start = ((), (), s32[]{:S(2)}) async-start(), calls=%async_computation.4 | async-start | bytes 4456448 | tf_op jit(solution)/shard_map/all_gather | solution.py:16
  7.9 222.9 %reduce-scatter.2.cloned.1.call-start = ((), (), s32[]{:S(2)}) async-start(), calls=%async_computation.5 | async-start | bytes 4456448 | tf_op jit(solution)/shard_map/reduce_scatter | solution.py:54
  93.1 0.7 copy-start.1
  93.1 1.5 copy-start.3
  93.1 7.2 %copy-start.2 = (s32[1,256]{1,0:T(1,128)S(1)}, s32[1,256]{1,0:T(1,128)}, u32[]{:S(2)}) copy-start(s32[1,256]{1,0:T(1,128)} %param.11) | copy-start | bytes 3076
  136.6 43.4 %all-to-all-start = ((s32[16,1,48]{2,1,0:T(1,128)}), s32[16,1,48]{2,1,0:T(1,128)S(1)}, u32[]{:S(2)}, u32[]{:S(2)}) async-start(s32[16,1,48]{2,1,0:T(1,128)} %bitcast.28), calls=%async_computation.1 | async-start | bytes 16384 | tf_op jit(solution)/shard_map/all_to_all | solution.py:41
  180.1 43.5 %all-to-all-start.1 = ((bf16[16,48,1024]{2,1,0:T(8,128)(2,1)}), bf16[16,48,1024]{2,1,0:T(8,128)(2,1)S(1)}, u32[]{:S(2)}, u32[]{:S(2)}) async-start(bf16[16,48,1024]{2,1,0:T(8,128)(2,1)} %scatter_fusion.1), calls=%async_computation.2 | async-start | bytes 3145728 | tf_op jit(solution)/shard_map/all_to_all | solution.py:40
  226.8 52.4 %all-to-all-start.2 = ((f32[16,1,48]{2,1,0:T(1,128)}), f32[16,1,48]{2,1,0:T(1,128)S(1)}, u32[]{:S(2)}, u32[]{:S(2)}) async-start(f32[16,1,48]{2,1,0:T(1,128)} %compare_select_fusion), calls=%async_computation.3 | async-start | bytes 16384 | tf_op jit(solution)/shard_map/all_to_all | solution.py:46
  230.8 51.6 %all-reduce.2.cloned.1.call-start = ((), (), s32[]{:S(2)}) async-start(), calls=%async_computation.6 | async-start | bytes 524288 | tf_op jit(solution)/shard_map/psum | solution.py:62
Sparse Core Ops, SparseCore 0:
  10.8 76.0 all-gather.1
  93.2 93.2 reduce-scatter.1
  233.9 21.2 all-reduce.1
where the time goes:
time: 295 us; the launch traced here: 291 us
  waiting for transfers between devices  108 us (37%)
  local copies, waits for them, and re-layouts  83.7 us (28%)
  blocking collectives  40.7 us (14%)
  other arithmetic  18.1 us (6%)
  starting transfers between devices  15.8 us (5%)
  between operations  14.5 us (5%)
  matrix products  9.99 us (3%)
    all_gather x1, waiting for transfers between devices, shards(): piece = lax.all_gather(expander, 'inner', axis=0, tiled=True)  76.9 us
    psum x1, blocking collectives, shards(): lax.psum(jnp.sum(masked.astype(jnp.float32), axis=0), ('inner', 'outer'))  40.7 us
    scatter x1, local copies, waits for them, and re-layouts, shards(): send_rows = jnp.zeros((group_size, capacity, expand_width), jnp.bfloat16)...  36.8 us
    scatter x1, local copies, waits for them, and re-layouts, shards(): jnp.zeros((group_size, capacity), jnp.int32).at[target_dev, slot_pos]  36.3 us
    all_to_all x1, waiting for transfers between devices, shards(): lax.all_to_all(send_rows, 'inner', split_axis=0, concat_axis=0, tiled=True)  29.5 us
    gather x3, other arithmetic, shards(): dest_count = counts[target_dev]  9.95 us
    all_to_all x1, starting transfers between devices, shards(): lax.all_to_all(send_rows, 'inner', split_axis=0, concat_axis=0, tiled=True)  6.53 us
  transfers between devices with their start and end apart: 6, of which 2 were waited for; matrix products, arithmetic and copies ran while one was open for 36% of the time, Pallas kernels for 0%

commit v1 on v0

v1 whole, which is shorter than its diff:
```python
import jax
import jax.numpy as jnp
from jax import lax
from jax.sharding import PartitionSpec as P


def shards(feats_first, feats_second, expander, tile_count, match_dev, match_tile):
    first_rows = feats_first[0]
    second_rows = feats_second[0]
    tile_rows = first_rows.shape[0]
    expand_width = expander.shape[1]
    group_size = lax.axis_size("inner")
    capacity = -(-max(2, 3 * tile_rows // group_size) // 16) * 16
    slots = group_size * capacity
    inner_pos = lax.axis_index("inner")
    outer_pos = lax.axis_index("outer")
    target_dev = match_dev[0, :, 0]
    target_tile = match_tile[0]
    row_index = jnp.arange(tile_rows, dtype=jnp.int32)
    same = (target_dev[:, None] == target_dev[None, :]) & (row_index[None, :] < row_index[:, None])
    slot_pos = jnp.sum(same.astype(jnp.int32), axis=1)
    slot = target_dev * capacity + slot_pos
    chosen = slot[:, None] == jnp.arange(slots, dtype=jnp.int32)[None, :]
    asked = jnp.sum(jnp.where(chosen, target_tile[:, None], 0), axis=0).reshape(group_size, capacity)
    wanted = lax.all_to_all(asked, "inner", split_axis=0, concat_axis=0, tiled=True).reshape(slots)
    piece = lax.all_gather(expander, "inner", axis=0, tiled=True)
    first_embed = jnp.dot(first_rows, piece, preferred_element_type=jnp.float32).astype(jnp.bfloat16)
    second_embed = jnp.dot(second_rows, piece, preferred_element_type=jnp.float32).astype(jnp.bfloat16)
    pick = (wanted[:, None] == row_index[None, :]).astype(jnp.bfloat16)
    send_rows = jnp.dot(pick, second_embed, preferred_element_type=jnp.float32).astype(jnp.bfloat16)
    recv_rows = lax.all_to_all(
        send_rows.reshape(group_size, capacity, expand_width), "inner", split_axis=0, concat_axis=0, tiled=True
    ).reshape(slots, expand_width)
    partner = jnp.dot(chosen.astype(jnp.bfloat16), recv_rows, preferred_element_type=jnp.float32)
    counts = lax.dynamic_index_in_dim(tile_count, outer_pos, 0, keepdims=False)
    own_count = lax.dynamic_index_in_dim(counts, inner_pos, 0, keepdims=False)
    live = row_index < own_count
    dest_count = jnp.sum(
        jnp.where(target_dev[:, None] == jnp.arange(group_size, dtype=jnp.int32)[None, :], counts[None, :], 0), axis=1
    )
    valid = live & (target_tile < dest_count)
    diff = first_embed.astype(jnp.float32) - partner
    invariance = jnp.where(valid, jnp.mean(diff * diff, axis=-1), jnp.float32(0.0))
    masked = jnp.where(live[:, None], first_embed, jnp.zeros_like(first_embed))
    column_total = lax.psum(jnp.sum(masked.astype(jnp.float32), axis=0), ("inner", "outer"))
    total = jnp.sum(tile_count).astype(jnp.float32)
    share_rows = expand_width // group_size
    local_share = lax.psum_scatter(
        lax.dot_general(masked, masked, (((0,), (0,)), ((), ())), preferred_element_type=jnp.float32),
        "inner",
        scatter_dimension=0,
        tiled=True,
    )
    gram_share = lax.psum(local_share, "outer")
    own_sums = lax.dynamic_slice_in_dim(column_total, inner_pos * share_rows, share_rows, 0)
    covariance = (gram_share - own_sums[:, None] * column_total[None, :] / total) / (total - 1.0)
    return (covariance, invariance[None, :])


def solution(mesh):
    return jax.shard_map(
        shards,
        mesh=mesh,
        in_specs=(
            P("outer", "inner", None),
            P("outer", "inner", None),
            P("inner", None),
            P(),
            P("outer", "inner", None),
            P("outer", "inner"),
        ),
        out_specs=(P("inner", None), P("outer", "inner")),
        check_vma=False,
    )
```

time: 295 us -> 240 us (0.81)
  local copies, waits for them, and re-layouts: 83.7 us -> 2.05 us
  blocking collectives: 40.7 us -> 80 us
  other arithmetic: 18.1 us -> 5.35 us
  starting transfers between devices: 15.8 us -> 5.72 us
  waiting for transfers between devices: 108 us -> 118 us
    scatter x2 -> x0, local copies, waits for them, and re-layouts: 73.1 us -> none  [the longest x1 36.8 us: shards(): send_rows = jnp.zeros((group_size, capacity, expand_width), jnp.bfloat16)...]
    psum x1, blocking collectives: 40.7 us -> 70.8 us  [shards(): lax.psum(jnp.sum(masked.astype(jnp.float32), axis=0), ('inner', 'outer'))]
    all_to_all x3 -> x1, waiting for transfers between devices: 29.5 us -> 0.01 us  [shards(): lax.all_to_all(send_rows.reshape(group_size, capacity, expand_width), 'in...]
    psum x1, waiting for transfers between devices: 0.01 us -> 22.2 us  [shards(): gram_share = lax.psum(local_share, 'outer')]
    reduce_scatter x1, waiting for transfers between devices: 0.02 us -> 18.5 us  [shards(): lax.psum_scatter(lax.dot_general(masked, masked, (((0,), (0,)), ((), ()))...]
    all_to_all x3 -> x1, starting transfers between devices: 15.7 us -> 5.61 us  [shards(): lax.all_to_all(send_rows.reshape(group_size, capacity, expand_width), 'in...]
    gather x4 -> x0, other arithmetic: 9.96 us -> none  [the longest x3 9.95 us: shards(): dest_count = counts[target_dev]]
    all_to_all x0 -> x1, blocking collectives: none -> 9.23 us  [shards(): lax.all_to_all(asked, 'inner', split_axis=0, concat_axis=0, tiled=True)]
  transfers between devices with their start and end apart: 6 -> 4, of which waited for: 2 -> 3; matrix products, arithmetic and copies ran while one was open for 36% -> 5% of each run, Pallas kernels for 0% -> 0%
where the time goes in v1:
time: 240 us; the launch traced here: 238 us
  waiting for transfers between devices  118 us (49%)
  blocking collectives  80 us (33%)
  between operations  14.5 us (6%)
  matrix products  12.4 us (5%)
  starting transfers between devices  5.72 us (2%)
  other arithmetic  5.35 us (2%)
    all_gather x1, waiting for transfers between devices, shards(): piece = lax.all_gather(expander, 'inner', axis=0, tiled=True)  77 us
    psum x1, blocking collectives, shards(): lax.psum(jnp.sum(masked.astype(jnp.float32), axis=0), ('inner', 'outer'))  70.8 us
    psum x1, waiting for transfers between devices, shards(): gram_share = lax.psum(local_share, 'outer')  22.2 us
    reduce_scatter x1, waiting for transfers between devices, shards(): lax.psum_scatter(lax.dot_general(masked, masked, (((0,), (0,)), ((), ()))...  18.5 us
    all_to_all x1, blocking collectives, shards(): lax.all_to_all(asked, 'inner', split_axis=0, concat_axis=0, tiled=True)  9.23 us
    all_to_all x1, starting transfers between devices, shards(): lax.all_to_all(send_rows.reshape(group_size, capacity, expand_width), 'in...  5.61 us
    dot_general x1, matrix products, shards(): jnp.dot(pick, second_embed, preferred_element_type=jnp.float32)  5.09 us
  transfers between devices with their start and end apart: 4, of which 3 were waited for; matrix products, arithmetic and copies ran while one was open for 5% of the time, Pallas kernels for 0%

profile of v1, /device:TPU:13, one launch (start us, length us, event | category | flops | bytes accessed | tf_op | source)
XLA Modules:
  0.0 238.4 jit_solution(4994649485600865249)
XLA Ops:
  7.2 0.0 copy-start
  7.2 0.0 all-gather.2.cloned.1.call-start
  7.2 0.7 all-gather.2.cloned.1.call-update
  7.9 0.0 reduce-scatter.2.cloned.1.call-start
  8.0 1.3 dynamic_slice.11
  9.2 0.6 iota_compare_fusion.6
  9.9 77.0 %all-gather.2.cloned.1.call-done = bf16[2048,1024]{1,0:T(8,128)(2,1)} async-done(((bf16[128,1024]{1,0:T(8,128)(2,1)}), bf16[2048,1024]{1,0:T(8,128)(2,1)}) %all-gather.2.cloned.1.call-update) | async-done | bytes 4194320 | tf_op jit(solution)/shard_map/all_gather | solution.py:26
  86.9 3.8 %convert_reduce_fusion = (f32[1024]{0:T(1024)S(1)}, bf16[256,1024]{1,0:T(8,128)(2,1)S(1)}) fusion(pred[256]{0:T(512)(128)(4,1)S(1)} %iota_compare_fusion.6, bf16[2048,1024]{1,0:T(8,128)(2,1)} %all-gather.2.cloned.1.call-done, bf16[1,256,2048]{2,1,0:T(8,128)(2,1)} %param.6), kind=kOutput, calls=%fused_computation.8 | convolution fusion | flops 1074789376 | bytes 5771520 | tf_op jit(solution)/shard_map/dot_general | solution.py:27
  90.6 0.0 copy-start.1
  90.6 0.0 copy-start.2
  90.7 2.8 %fusion.8 = f32[1024,1024]{1,0:T(8,128)} fusion(bf16[256,1024]{1,0:T(8,128)(2,1)S(1)} %get-tuple-element.3, pred[256]{0:T(512)(128)(4,1)S(1)} %iota_compare_fusion.6), kind=kOutput, calls=%fused_computation.19 | convolution fusion | flops 537133056 | bytes 4718848 | tf_op jit(solution)/shard_map/dot_general | solution.py:49
  93.4 0.0 reduce-scatter.2.cloned.1.call-update
  93.5 0.0 copy-done.1
  93.5 0.2 convert_reduce_fusion.1
  93.7 0.0 copy-done.2
  93.7 0.2 select_reduce_fusion
  93.8 0.1 all_to_all.9
  93.9 9.2 %all_to_all.14 = s32[16,1,48]{2,1,0:T(1,128)S(1)} all-to-all(s32[16,1,48]{2,1,0:T(1,128)S(1)} %all_to_all.9), channel_id=1, replica_groups=mesh['inner'=16,'outer'=2] {'inner'}, dimensions={0} | all-to-all | bytes 6144 | tf_op jit(solution)/shard_map/all_to_all | solution.py:25
  103.2 0.5 broadcast.32
  103.7 0.7 reduce.3
  104.3 0.1 eq.66
  104.4 0.0 copy-done
  104.4 0.0 copy-start.3
  104.4 5.1 %convolution_convert_fusion = bf16[768,1024]{1,0:T(8,128)(2,1)} fusion(bf16[2048,1024]{1,0:T(8,128)(2,1)} %all-gather.2.cloned.1.call-done, bf16[1,256,2048]{2,1,0:T(8,128)(2,1)S(1)} %copy-done, s32[768]{0:T(1024)S(1)} %eq.66), kind=kOutput, calls=%fused_computation | convolution fusion | flops 1477640192 | bytes 6818816 | tf_op jit(solution)/shard_map/dot_general | solution.py:30
  109.5 5.6 %all-to-all-start.1 = ((bf16[16,48,1024]{2,1,0:T(8,128)(2,1)}), bf16[16,48,1024]{2,1,0:T(8,128)(2,1)S(1)}, u32[]{:S(2)}, u32[]{:S(2)}) async-start(bf16[16,48,1024]{2,1,0:T(8,128)(2,1)} %bitcast.22), calls=%async_computation.2 | async-start | bytes 3145728 | tf_op jit(solution)/shard_map/all_to_all | solution.py:31
  115.1 0.0 all-reduce.2.cloned.1.call-start
  115.2 0.0 copy-done.3
  115.2 0.6 reduce_sum.57
  116.5 0.1 select_reduce_fusion.1
  116.6 70.8 %psum.15 = f32[1024]{0:T(1024)S(1)} all-reduce(f32[1024]{0:T(1024)S(1)} %get-tuple-element.2), channel_id=1, replica_groups=mesh['inner'=16,'outer'=2] {'inner','outer'}, use_global_device_ids=true, to_apply=%region_3.4 | all-reduce | flops 1024 | bytes 8192 | tf_op jit(solution)/shard_map/psum | solution.py:45
  187.4 0.1 dynamic_slice.12
  187.4 0.0 all-to-all-done.1
  187.4 0.7 fusion.1
  188.2 18.5 %reduce-scatter.2.cloned.1.call-done = f32[64,1024]{1,0:T(8,128)} async-done(((f32[1024,1024]{1,0:T(8,128)}), f32[64,1024]{1,0:T(8,128)}) %reduce-scatter.2.cloned.1.call-update) | async-done | bytes 262160 | tf_op jit(solution)/shard_map/reduce_scatter | solution.py:48
  206.7 0.0 all-reduce.2.cloned.1.call-update
  206.7 1.2 and_select_fusion
  207.9 22.2 %all-reduce.2.cloned.1.call-done = f32[64,1024]{1,0:T(8,128)} async-done(((f32[64,1024]{1,0:T(8,128)}), f32[64,1024]{1,0:T(8,128)}) %all-reduce.2.cloned.1.call-update) | async-done | bytes 262160 | tf_op jit(solution)/shard_map/psum | solution.py:54
  230.1 1.8 subtract_divide_fusion
  (3 shorter events, 0.0 us)
Async XLA Ops:
  7.2 97.3 %copy-start = (bf16[1,256,2048]{2,1,0:T(8,128)(2,1)S(1)}, bf16[1,256,2048]{2,1,0:T(8,128)(2,1)}, u32[]{:S(2)}) copy-start(bf16[1,256,2048]{2,1,0:T(8,128)(2,1)} %param.7) | copy-start | bytes 3145732
  7.2 79.7 %all-gather.2.cloned.1.call-start = ((), (), s32[]{:S(2)}) async-start(), calls=%async_computation.3 | async-start | bytes 4456448 | tf_op jit(solution)/shard_map/all_gather | solution.py:26
  7.9 198.8 %reduce-scatter.2.cloned.1.call-start = ((), (), s32[]{:S(2)}) async-start(), calls=%async_computation.4 | async-start | bytes 4456448 | tf_op jit(solution)/shard_map/reduce_scatter | solution.py:48
  90.6 2.8 %copy-start.1 = (s32[1,256,1]{1,2,0:T(1,128)S(1)}, s32[1,256,1]{1,2,0:T(1,128)}, u32[]{:S(2)}) copy-start(s32[1,256,1]{1,2,0:T(1,128)} %param.10) | copy-start | bytes 3076
  90.6 3.0 %copy-start.2 = (s32[1,256]{1,0:T(1,128)S(1)}, s32[1,256]{1,0:T(1,128)}, u32[]{:S(2)}) copy-start(s32[1,256]{1,0:T(1,128)} %param.11) | copy-start | bytes 3076
  104.4 10.8 %copy-start.3 = (s32[2,16]{1,0:T(2,128)S(1)}, s32[2,16]{1,0:T(2,128)}, u32[]{:S(2)}) copy-start(s32[2,16]{1,0:T(2,128)} %param.9) | copy-start | bytes 388
  109.5 77.9 %all-to-all-start.1 = ((bf16[16,48,1024]{2,1,0:T(8,128)(2,1)}), bf16[16,48,1024]{2,1,0:T(8,128)(2,1)S(1)}, u32[]{:S(2)}, u32[]{:S(2)}) async-start(bf16[16,48,1024]{2,1,0:T(8,128)(2,1)} %bitcast.22), calls=%async_computation.2 | async-start | bytes 3145728 | tf_op jit(solution)/shard_map/all_to_all | solution.py:31
  115.1 115.0 %all-reduce.2.cloned.1.call-start = ((), (), s32[]{:S(2)}) async-start(), calls=%async_computation.5 | async-start | bytes 524288 | tf_op jit(solution)/shard_map/psum | solution.py:54
Sparse Core Ops, SparseCore 0:
  10.8 76.0 all-gather.1
  93.6 113.0 reduce-scatter.1
  209.0 21.0 all-reduce.1

commit v2 on v1

v2 whole, which is shorter than its diff:
```python
import functools

import jax
import jax.numpy as jnp
from jax import lax
from jax.experimental import pallas as pl
from jax.experimental.pallas import tpu as pltpu
from jax.sharding import PartitionSpec as P

MESH = pl.DeviceIdType.MESH


def minor_size(n):
    return 4 if n % 4 == 0 and n > 4 else 1


def greet(n, m):
    me, core = lax.axis_index("inner"), lax.axis_index("outer")
    barrier = pltpu.get_barrier_semaphore()

    def inner(k, c):
        pl.semaphore_signal(barrier, inc=1, device_id={"inner": lax.rem(me + k, n)}, device_id_type=MESH)
        return c

    lax.fori_loop(1, n, inner, 0)
    for t in range(1, m):
        pl.semaphore_signal(barrier, inc=1, device_id={"outer": lax.rem(core + t, m)}, device_id_type=MESH)
    pl.semaphore_wait(barrier, n - 1 + m - 1)


def remote(src, dst, sems, at, device):
    return pltpu.make_async_remote_copy(
        src_ref=src,
        dst_ref=dst,
        send_sem=sems[0].at[at],
        recv_sem=sems[1].at[at],
        device_id=device,
        device_id_type=MESH,
    )


def each(low, high, body):
    def step(k, c):
        body(k)
        return c

    lax.fori_loop(low, high, step, 0)


def gather_kernel(n, m, w, ask, full, got, zs, zr, ps, pr, os, orr, qs, qr):
    me, core = lax.axis_index("inner"), lax.axis_index("outer")
    minor = minor_size(n)
    major = n // minor
    a, b = me // minor, lax.rem(me, minor)
    part = w.shape[1] // m

    def cols(t):
        return pl.ds(pl.multiple_of(t * part, 128), part)

    mine = cols(core)
    greet(n, m)

    def z_copy(k, index):
        peer = lax.rem(a + k, major) * minor + b
        return remote(w.at[:, mine], full.at[index, :, mine], (zs, zr), k, {"inner": peer})

    def p_copy(k, j, index):
        peer = a * minor + lax.rem(b + j, minor)
        source = w.at[:, mine] if k is None else full.at[index, :, mine]
        at = j if k is None else k * minor + j
        return remote(source, full.at[index, :, mine], (ps, pr), at, {"inner": peer})

    def o_copy(t, index, at, lanes):
        block = full.at[index, :, lanes]
        return remote(block, block, (os, orr), t * n + at, {"outer": lax.rem(core + t, m)})

    def q_copy(k, index):
        return remote(ask.at[lax.rem(me + k, n)], got.at[index], (qs, qr), k, {"inner": lax.rem(me + k, n)})

    def block_of(k, j):
        return lax.rem(a - k + major, major) * minor + lax.rem(b - j + minor, minor)

    each(1, major, lambda k: z_copy(k, me).start())
    for j in range(1, minor):
        p_copy(None, j, me).start()
    each(1, n, lambda k: q_copy(k, me).start())
    full[me] = w[...]
    got[me] = ask[me]

    def relay(k):
        index = block_of(k, 0)
        z_copy(k, index).wait_recv()
        for j in range(1, minor):
            p_copy(k, j, index).start()
        for t in range(1, m):
            o_copy(t, index, k * minor, mine).start()

    each(1, major, relay)

    def share(k):
        for j in range(1, minor):
            index = block_of(k, j)
            p_copy(k, j, index).wait_recv()
            for t in range(1, m):
                o_copy(t, index, k * minor + j, mine).start()

    each(0, major, share)

    def settle(k):
        for j in range(minor):
            for t in range(1, m):
                copy = o_copy(t, block_of(k, j), k * minor + j, cols(lax.rem(core - t + m, m)))
                if j == 0:

                    @pl.when(k > 0)
                    def _():
                        copy.wait_recv()
                        copy.wait_send()
                else:
                    copy.wait_recv()
                    copy.wait_send()
            if j > 0:
                p_copy(k, j, block_of(k, 0)).wait_send()

    each(0, major, settle)
    each(1, major, lambda k: z_copy(k, me).wait_send())

    def questions(k):
        copy = q_copy(k, lax.rem(me - k + n, n))
        copy.wait_recv()
        copy.wait_send()

    each(1, n, questions)


def gather(expander, asked, n, m):
    depth, width = expander.shape
    dma = pltpu.SemaphoreType.DMA
    minor = minor_size(n)
    vmem = pl.BlockSpec(memory_space=pltpu.VMEM)
    return pl.pallas_call(
        functools.partial(gather_kernel, n, m),
        out_shape=(
            jax.ShapeDtypeStruct((n, depth, width), expander.dtype),
            jax.ShapeDtypeStruct(asked.shape, asked.dtype),
        ),
        in_specs=[vmem] * 2,
        out_specs=(vmem, vmem),
        scratch_shapes=[
            dma((n // minor,)), dma((n // minor,)), dma((n,)), dma((n,)), dma((m * n,)), dma((m * n,)), dma((n,)), dma((n,)),
        ],
        compiler_params=pltpu.CompilerParams(collective_id=0, has_side_effects=True, vmem_limit_bytes=40 << 20),
        name="gather",
    )(expander, asked)


def exchange_kernel(n, m, rows, gram, sums, got, out, total, landed, half, plane, line, last,
                    s_core, s_all, rs, rr, os, orr, ps, pr, zs, zr, fs, fr, cs, cr, ss, sr):
    me, core = lax.axis_index("inner"), lax.axis_index("outer")
    minor = minor_size(n)
    major = n // minor
    a, b = me // minor, lax.rem(me, minor)
    part = out.shape[1] // m

    def cols(t):
        return pl.ds(pl.multiple_of(t * part, 128), part)

    mine = cols(core)
    greet(n, m)

    def o_copy(t):
        peer = lax.rem(core + t, m)
        return remote(gram.at[:, :, :, cols(peer)], landed.at[t], (os, orr), t, {"outer": peer})

    def c_copy(t, index):
        return remote(sums, s_core.at[index], (cs, cr), t, {"outer": lax.rem(core + t, m)})

    def r_copy(k, index):
        peer = lax.rem(me + k, n)
        return remote(rows.at[peer], got.at[index], (rs, rr), k, {"inner": peer})

    def p_copy(j):
        other = lax.rem(b + j, minor)
        return remote(half.at[:, other], plane.at[j], (ps, pr), j, {"inner": a * minor + other})

    def z_copy(k):
        other = lax.rem(a + k, major)
        return remote(line.at[other], last.at[k], (zs, zr), k, {"inner": other * minor + b})

    def s_copy(k, index):
        return remote(s_all.at[index], s_all.at[index], (ss, sr), k, {"inner": lax.rem(me + k, n)})

    def f_copy(t, lanes):
        return remote(out.at[:, lanes], out.at[:, lanes], (fs, fr), t, {"outer": lax.rem(core + t, m)})

    for t in range(1, m):
        c_copy(t, core).start()
        o_copy(t).start()
    each(1, n, lambda k: r_copy(k, me).start())
    got[me] = rows[me]
    s_core[core] = sums[...]
    for t in range(1, m):
        c_copy(t, lax.rem(core - t + m, m)).wait_recv()
    s_all[me] = functools.reduce(lambda x, y: x + y, [s_core[t] for t in range(m)])
    each(1, n, lambda k: s_copy(k, me).start())
    for t in range(1, m):
        o_copy(t).wait_recv()

    def add_cores(i):
        x, y = i // minor, lax.rem(i, minor)
        value = gram[x, y, :, mine]
        for t in range(1, m):
            value = value + landed[t, x, y]
        half[x, y] = value

    each(0, n, add_cores)
    for j in range(1, minor):
        p_copy(j).start()
    for j in range(1, minor):
        p_copy(j).wait_recv()

    def add_plane(x):
        value = half[x, b]
        for j in range(1, minor):
            value = value + plane[j, x]
        line[x] = value

    each(0, major, add_plane)
    each(1, major, lambda k: z_copy(k).start())
    each(1, major, lambda k: z_copy(k).wait_recv())
    value = line[a]
    for k in range(1, major):
        value = value + last[k]
    out[:, mine] = value
    for t in range(1, m):
        f_copy(t, mine).start()
    each(1, n, lambda k: s_copy(k, lax.rem(me - k + n, n)).wait_recv())
    value = s_all[0]
    for k in range(1, n):
        value = value + s_all[k]
    total[...] = value

    def settle(k):
        r_copy(k, lax.rem(me - k + n, n)).wait_recv()
        r_copy(k, me).wait_send()
        s_copy(k, me).wait_send()

    each(1, n, settle)
    for t in range(1, m):
        f_copy(t, cols(lax.rem(core - t + m, m))).wait_recv()
        f_copy(t, mine).wait_send()
        o_copy(t).wait_send()
        c_copy(t, core).wait_send()
    for j in range(1, minor):
        p_copy(j).wait_send()
    each(1, major, lambda k: z_copy(k).wait_send())


def exchange(rows, gram, sums, n, m):
    width = gram.shape[1]
    share, part = width // n, width // m
    minor = minor_size(n)
    major = n // minor
    dma = pltpu.SemaphoreType.DMA
    vmem = pl.BlockSpec(memory_space=pltpu.VMEM)
    f32 = jnp.float32
    pairs = [n, m, minor, major, m, m, n]
    return pl.pallas_call(
        functools.partial(exchange_kernel, n, m),
        out_shape=(
            jax.ShapeDtypeStruct(rows.shape, rows.dtype),
            jax.ShapeDtypeStruct((share, width), f32),
            jax.ShapeDtypeStruct((1, width), f32),
        ),
        in_specs=[vmem] * 3,
        out_specs=(vmem,) * 3,
        scratch_shapes=[
            pltpu.VMEM((m, major, minor, share, part), f32),
            pltpu.VMEM((major, minor, share, part), f32),
            pltpu.VMEM((minor, major, share, part), f32),
            pltpu.VMEM((major, share, part), f32),
            pltpu.VMEM((major, share, part), f32),
            pltpu.VMEM((m, 1, width), f32),
            pltpu.VMEM((n, 1, width), f32),
        ]
        + [dma((size,)) for size in pairs for _ in range(2)],
        compiler_params=pltpu.CompilerParams(collective_id=1, has_side_effects=True, vmem_limit_bytes=40 << 20),
        name="exchange",
    )(rows, gram.reshape(major, minor, share, width), sums)


def shards(feats_first, feats_second, expander, tile_count, match_dev, match_tile):
    first_rows = feats_first[0]
    second_rows = feats_second[0]
    tile_rows = first_rows.shape[0]
    expand_width = expander.shape[1]
    group_size = lax.axis_size("inner")
    capacity = -(-max(2, 3 * tile_rows // group_size) // 16) * 16
    slots = group_size * capacity
    inner_pos = lax.axis_index("inner")
    outer_pos = lax.axis_index("outer")
    target_dev = match_dev[0, :, 0]
    target_tile = match_tile[0]
    row_index = jnp.arange(tile_rows, dtype=jnp.int32)
    same = (target_dev[:, None] == target_dev[None, :]) & (row_index[None, :] < row_index[:, None])
    slot_pos = jnp.sum(same.astype(jnp.int32), axis=1)
    slot = target_dev * capacity + slot_pos
    chosen = slot[:, None] == jnp.arange(slots, dtype=jnp.int32)[None, :]
    padded = -(-capacity // 128) * 128
    asked = jnp.sum(jnp.where(chosen, target_tile[:, None], 0), axis=0).reshape(group_size, 1, capacity)
    asked = jnp.pad(asked, ((0, 0), (0, 0), (0, padded - capacity)))
    piece, wanted = gather(expander, asked, group_size, lax.axis_size("outer"))
    piece = piece.reshape(-1, expand_width)
    wanted = wanted[:, 0, :capacity].reshape(slots)
    first_embed = jnp.dot(first_rows, piece, preferred_element_type=jnp.float32).astype(jnp.bfloat16)
    second_embed = jnp.dot(second_rows, piece, preferred_element_type=jnp.float32).astype(jnp.bfloat16)
    pick = (wanted[:, None] == row_index[None, :]).astype(jnp.bfloat16)
    send_rows = jnp.dot(pick, second_embed, preferred_element_type=jnp.float32).astype(jnp.bfloat16)
    counts = lax.dynamic_index_in_dim(tile_count, outer_pos, 0, keepdims=False)
    own_count = lax.dynamic_index_in_dim(counts, inner_pos, 0, keepdims=False)
    live = row_index < own_count
    masked = jnp.where(live[:, None], first_embed, jnp.zeros_like(first_embed))
    gram = lax.dot_general(masked, masked, (((0,), (0,)), ((), ())), preferred_element_type=jnp.float32)
    recv_rows, gram_share, column_total = exchange(
        send_rows.reshape(group_size, capacity, expand_width),
        gram,
        jnp.sum(masked.astype(jnp.float32), axis=0, keepdims=True),
        group_size,
        lax.axis_size("outer"),
    )
    recv_rows = recv_rows.reshape(slots, expand_width)
    column_total = column_total[0]
    partner = jnp.dot(chosen.astype(jnp.bfloat16), recv_rows, preferred_element_type=jnp.float32)
    dest_count = jnp.sum(
        jnp.where(target_dev[:, None] == jnp.arange(group_size, dtype=jnp.int32)[None, :], counts[None, :], 0), axis=1
    )
    valid = live & (target_tile < dest_count)
    diff = first_embed.astype(jnp.float32) - partner
    invariance = jnp.where(valid, jnp.mean(diff * diff, axis=-1), jnp.float32(0.0))
    total = jnp.sum(tile_count).astype(jnp.float32)
    share_rows = expand_width // group_size
    own_sums = lax.dynamic_slice_in_dim(column_total, inner_pos * share_rows, share_rows, 0)
    covariance = (gram_share - own_sums[:, None] * column_total[None, :] / total) / (total - 1.0)
    return (covariance, invariance[None, :])


def solution(mesh):
    return jax.shard_map(
        shards,
        mesh=mesh,
        in_specs=(
            P("outer", "inner", None),
            P("outer", "inner", None),
            P("inner", None),
            P(),
            P("outer", "inner", None),
            P("outer", "inner"),
        ),
        out_specs=(P("inner", None), P("outer", "inner")),
        check_vma=False,
    )
```

time: 240 us -> 118 us (0.49)
  waiting for transfers between devices: 118 us -> 0 us
  Pallas kernels: 0 us -> 94.6 us
  blocking collectives: 80 us -> 0 us
  between operations: 14.5 us -> 1.45 us
  starting transfers between devices: 5.72 us -> 0 us
  local copies, waits for them, and re-layouts: 2.05 us -> 4.91 us
    pallas_call x0 -> x2, Pallas kernels: none -> 94.6 us  [the longest x1 63.6 us: exchange(): pl.pallas_call(functools.partial(exchange_kernel, n, m), out_shape=(jax.S...]
    all_gather x1 -> x0, waiting for transfers between devices: 77 us -> none  [shards(): piece = lax.all_gather(expander, 'inner', axis=0, tiled=True)]
    psum x1 -> x0, blocking collectives: 70.8 us -> none  [shards(): lax.psum(jnp.sum(masked.astype(jnp.float32), axis=0), ('inner', 'outer'))]
    psum x1 -> x0, waiting for transfers between devices: 22.2 us -> none  [shards(): gram_share = lax.psum(local_share, 'outer')]
    reduce_scatter x1 -> x0, waiting for transfers between devices: 18.5 us -> none  [shards(): lax.psum_scatter(lax.dot_general(masked, masked, (((0,), (0,)), ((), ()))...]
    all_to_all x1 -> x0, blocking collectives: 9.23 us -> none  [shards(): lax.all_to_all(asked, 'inner', split_axis=0, concat_axis=0, tiled=True)]
    all_to_all x1 -> x0, starting transfers between devices: 5.61 us -> none  [shards(): lax.all_to_all(send_rows.reshape(group_size, capacity, expand_width), 'in...]
    unnamed x8 -> x14, local copies, waits for them, and re-layouts: 0.03 us -> 4.04 us
  transfers between devices with their start and end apart: 4 -> 0, of which waited for: 3 -> 0; matrix products, arithmetic and copies ran while one was open for 5% -> 0% of each run, Pallas kernels for 0% -> 0%
where the time goes in v2:
time: 118 us
  Pallas kernels  94.6 us (80%)
  matrix products  11.5 us (10%)
  other arithmetic  5.81 us (5%)
  local copies, waits for them, and re-layouts  4.91 us (4%)
  between operations  1.45 us (1%)
    pallas_call x1, Pallas kernels, exchange(): pl.pallas_call(functools.partial(exchange_kernel, n, m), out_shape=(jax.S...  63.6 us
    pallas_call x1, Pallas kernels, gather(): pl.pallas_call(functools.partial(gather_kernel, n, m), out_shape=(jax.Sha...  31 us
    dot_general x1, matrix products, shards(): jnp.dot(pick, second_embed, preferred_element_type=jnp.float32)  4.6 us
    unnamed x14, local copies, waits for them, and re-layouts  4.04 us
    dot_general x1, matrix products, shards(): jnp.dot(first_rows, piece, preferred_element_type=jnp.float32)  3.88 us

profile of v2, /device:TPU:13, one launch (start us, length us, event | category | flops | bytes accessed | tf_op | source)
XLA Modules:
  0.0 118.2 jit_solution(2896797825486907220)
XLA Ops:
  0.6 0.0 copy-start
  0.6 1.0 convert_reduce_fusion.1
  1.6 0.7 multiply_add_fusion
  2.3 0.8 select_reduce_fusion
  3.1 0.1 reshape.57
  3.2 0.0 copy-start.1
  3.2 0.9 copy-done.1
  4.2 31.0 %gather.1 = (bf16[16,128,1024]{2,1,0:T(8,128)(2,1)S(1)}, s32[16,1,128]{2,1,0:T(1,128)S(1)}) custom-call(bf16[128,1024]{1,0:T(8,128)(2,1)S(1)} %copy-done.1, s32[16,1,128]{2,1,0:T(1,128)S(1)} %pad.4.ask), custom_call_target="tpu_custom_call" | custom-call | tf_op jit(solution)/shard_map/gather/pallas_call | solution.py:141
  35.2 0.0 copy-start.2
  35.2 1.9 %copy-done.2 = bf16[16,128,1024]{2,1,0:T(8,128)(2,1)} copy-done((bf16[16,128,1024]{2,1,0:T(8,128)(2,1)}, bf16[16,128,1024]{2,1,0:T(8,128)(2,1)S(1)}, u32[]{:S(2)}) %copy-start.2) | copy-done | bytes 4194328
  37.1 0.1 eq.60
  37.2 0.0 copy-done
  37.2 0.0 copy-start.6
  37.2 4.6 %convolution_convert_fusion = bf16[768,1024]{1,0:T(8,128)(2,1)S(1)} fusion(bf16[2048,1024]{1,0:T(8,128)(2,1)} %bitcast.33, bf16[1,256,2048]{2,1,0:T(8,128)(2,1)S(1)} %copy-done, s32[768]{0:T(1024)S(1)} %eq.60), kind=kOutput, calls=%fused_computation | convolution fusion | flops 1477640192 | bytes 6818816 | tf_op jit(solution)/shard_map/dot_general | solution.py:318
  41.8 0.0 copy-done.6
  41.8 0.6 dynamic_slice.11
  42.4 0.6 iota_compare_fusion.6
  43.0 3.9 %convert_reduce_fusion = (f32[1024]{0:T(1024)S(1)}, bf16[1024,256]{1,0:T(8,128)(2,1)S(1)}) fusion(pred[256]{0:T(512)(128)(4,1)S(1)} %iota_compare_fusion.6, bf16[2048,1024]{1,0:T(8,128)(2,1)} %bitcast.34, bf16[1,256,2048]{2,1,0:T(8,128)(2,1)} %param.6), kind=kOutput, calls=%fused_computation.8 | convolution fusion | flops 1074789376 | bytes 5771520 | tf_op jit(solution)/shard_map/dot_general | solution.py:315
  46.9 0.7 fusion.5
  47.7 0.0 copy-start.4
  47.7 0.0 copy-start.5
  47.7 63.6 %exchange.1 = (bf16[16,48,1024]{2,1,0:T(8,128)(2,1)S(1)}, f32[64,1024]{1,0:T(8,128)S(1)}, f32[1,1024]{1,0:T(1,128)S(1)}) custom-call(bf16[16,48,1024]{2,1,0:T(8,128)(2,1)S(1)} %bitcast.30, f32[4,4,64,1024]{3,2,1,0:T(8,128)S(1)} %bitcast.29, f32[1,1024]{1,0:T(1,128)S(1)} %bitcast.32), custom_call_target="tpu_custom_call" | custom-call | tf_op jit(solution)/shard_map/exchange/pallas_call | solution.py:268
  111.3 0.0 copy-start.3
  111.3 1.1 copy-done.3
  112.5 0.6 reduce_sum.59
  113.8 0.1 dynamic-slice_bitcast_fusion.1
  113.8 0.8 subtract_divide_fusion
  114.7 2.2 %fusion.1 = f32[256]{0:T(256)S(1)} fusion(bf16[768,1024]{1,0:T(8,128)(2,1)} %bitcast.35, bf16[1024,256]{1,0:T(8,128)(2,1)S(1)} %get-tuple-element.13, s32[256]{0:T(256)S(1)} %multiply_add_fusion), kind=kOutput, calls=%fused_computation.5 | convolution fusion | flops 403898112 | bytes 2099200 | tf_op jit(solution)/shard_map/dot_general | solution.py:333
  116.9 0.0 copy-done.4
  116.9 0.1 select_reduce_fusion.1
  117.0 0.0 copy-done.5
  117.0 1.2 %and_select_fusion = f32[1,256]{1,0:T(1,128)} fusion(f32[1,256]{1,0:T(1,128)S(1)} %bitcast.39, s32[1,256]{1,0:T(1,128)S(1)} %copy-done.5, s32[1,256]{1,0:T(1,128)S(1)} %bitcast.40, s32[]{:T(128)} %bitcast.5), kind=kLoop, calls=%fused_computation.24 | loop fusion | flops 1024 | bytes 4100 | tf_op jit(solution)/shard_map/jit(_where)/select_n | solution.py:339
  (4 shorter events, 0.0 us)
Async XLA Ops:
  0.6 36.6 %copy-start = (bf16[1,256,2048]{2,1,0:T(8,128)(2,1)S(1)}, bf16[1,256,2048]{2,1,0:T(8,128)(2,1)}, u32[]{:S(2)}) copy-start(bf16[1,256,2048]{2,1,0:T(8,128)(2,1)} %param.7) | copy-start | bytes 3145732
  3.2 1.0 copy-start.1
  35.2 1.9 %copy-start.2 = (bf16[16,128,1024]{2,1,0:T(8,128)(2,1)}, bf16[16,128,1024]{2,1,0:T(8,128)(2,1)S(1)}, u32[]{:S(2)}) copy-start(bf16[16,128,1024]{2,1,0:T(8,128)(2,1)S(1)} %get-tuple-element.8) | copy-start | bytes 12582916
  37.2 4.6 %copy-start.6 = (s32[2,16]{1,0:T(2,128)S(1)}, s32[2,16]{1,0:T(2,128)}, u32[]{:S(2)}) copy-start(s32[2,16]{1,0:T(2,128)} %param.9) | copy-start | bytes 388
  47.7 69.2 %copy-start.4 = (s32[1,256,1]{1,2,0:T(1,128)S(1)}, s32[1,256,1]{1,2,0:T(1,128)}, u32[]{:S(2)}) copy-start(s32[1,256,1]{1,2,0:T(1,128)} %param.10) | copy-start | bytes 3076
  47.7 69.3 %copy-start.5 = (s32[1,256]{1,0:T(1,128)S(1)}, s32[1,256]{1,0:T(1,128)}, u32[]{:S(2)}) copy-start(s32[1,256]{1,0:T(1,128)} %param.11) | copy-start | bytes 3076
  111.3 1.2 copy-start.3

commit v3 on v2

--- a/solution.py
+++ b/solution.py
@@ -47,83 +47,127 @@
     lax.fori_loop(low, high, step, 0)
 
 
-def gather_kernel(n, m, w, ask, full, got, zs, zr, ps, pr, os, orr, qs, qr):
+def gather_kernel(n, m, w, ask, first, second, got, first_embed, second_embed, full, feats, acc,
+                  zs, zr, ps, pr, os, orr, qs, qr, loads):
     me, core = lax.axis_index("inner"), lax.axis_index("outer")
     minor = minor_size(n)
     major = n // minor
     a, b = me // minor, lax.rem(me, minor)
-    part = w.shape[1] // m
+    depth, width = w.shape
+    part = width // m
+    chunk = minor * depth
+    lanes = min(width, 256)
 
     def cols(t):
         return pl.ds(pl.multiple_of(t * part, 128), part)
 
+    def block(x, y, columns):
+        return full.at[x, pl.ds(pl.multiple_of(y * depth, depth), depth), columns]
+
     mine = cols(core)
     greet(n, m)
 
-    def z_copy(k, index):
+    def z_copy(k, x):
         peer = lax.rem(a + k, major) * minor + b
-        return remote(w.at[:, mine], full.at[index, :, mine], (zs, zr), k, {"inner": peer})
-
-    def p_copy(k, j, index):
+        return remote(w.at[:, mine], block(x, b, mine), (zs, zr), k, {"inner": peer})
+
+    def p_copy(k, j, x, y):
         peer = a * minor + lax.rem(b + j, minor)
-        source = w.at[:, mine] if k is None else full.at[index, :, mine]
+        source = w.at[:, mine] if k is None else block(x, y, mine)
         at = j if k is None else k * minor + j
-        return remote(source, full.at[index, :, mine], (ps, pr), at, {"inner": peer})
-
-    def o_copy(t, index, at, lanes):
-        block = full.at[index, :, lanes]
-        return remote(block, block, (os, orr), t * n + at, {"outer": lax.rem(core + t, m)})
+        return remote(source, block(x, y, mine), (ps, pr), at, {"inner": peer})
+
+    def o_copy(t, x, y, at, columns):
+        return remote(
+            block(x, y, columns), block(x, y, columns), (os, orr), t * n + at, {"outer": lax.rem(core + t, m)}
+        )
 
     def q_copy(k, index):
         return remote(ask.at[lax.rem(me + k, n)], got.at[index], (qs, qr), k, {"inner": lax.rem(me + k, n)})
 
-    def block_of(k, j):
-        return lax.rem(a - k + major, major) * minor + lax.rem(b - j + minor, minor)
-
-    each(1, major, lambda k: z_copy(k, me).start())
+    def plane(k):
+        return lax.rem(a - k + major, major)
+
+    def column(j):
+        return lax.rem(b - j + minor, minor)
+
+    each(1, major, lambda k: z_copy(k, a).start())
     for j in range(1, minor):
-        p_copy(None, j, me).start()
+        p_copy(None, j, a, b).start()
+    fetch = [pltpu.make_async_copy(ref, feats.at[i], loads.at[i]) for i, ref in enumerate((first, second))]
+    for copy in fetch:
+        copy.start()
     each(1, n, lambda k: q_copy(k, me).start())
-    full[me] = w[...]
+    full[a, pl.ds(pl.multiple_of(b * depth, depth), depth), :] = w[...]
     got[me] = ask[me]
+    acc[...] = jnp.zeros_like(acc)
 
     def relay(k):
-        index = block_of(k, 0)
-        z_copy(k, index).wait_recv()
+        x = plane(k)
+        z_copy(k, x).wait_recv()
         for j in range(1, minor):
-            p_copy(k, j, index).start()
+            p_copy(k, j, x, b).start()
         for t in range(1, m):
-            o_copy(t, index, k * minor, mine).start()
+            o_copy(t, x, b, k * minor, mine).start()
 
     each(1, major, relay)
 
     def share(k):
         for j in range(1, minor):
-            index = block_of(k, j)
-            p_copy(k, j, index).wait_recv()
+            p_copy(k, j, plane(k), column(j)).wait_recv()
             for t in range(1, m):
-                o_copy(t, index, k * minor + j, mine).start()
-
-    each(0, major, share)
+                o_copy(t, plane(k), column(j), k * minor + j, mine).start()
+
+    def multiply(k):
+        x = plane(k)
+        for j in range(minor):
+            for t in range(1, m):
+                copy = o_copy(t, x, column(j), k * minor + j, cols(lax.rem(core - t + m, m)))
+                if j == 0:
+
+                    @pl.when(k > 0)
+                    def _():
+                        copy.wait_recv()
+                else:
+                    copy.wait_recv()
+        deep = pl.ds(pl.multiple_of(x * chunk, 128), chunk)
+
+        def columns(c):
+            at = pl.ds(pl.multiple_of(c * lanes, lanes), lanes)
+            for i in range(2):
+                acc[i, :, at] += jnp.dot(feats[i, :, deep], full[x, :, at], preferred_element_type=jnp.float32)
+
+        each(0, width // lanes, columns)
+
+    share(0)
+    for copy in fetch:
+        copy.wait()
+
+    def steps(k):
+        share(k)
+        multiply(k - 1)
+
+    each(1, major, steps)
+    multiply(major - 1)
+    first_embed[...] = acc[0].astype(first_embed.dtype)
+    second_embed[...] = acc[1].astype(second_embed.dtype)
 
     def settle(k):
         for j in range(minor):
             for t in range(1, m):
-                copy = o_copy(t, block_of(k, j), k * minor + j, cols(lax.rem(core - t + m, m)))
+                copy = o_copy(t, plane(k), column(j), k * minor + j, mine)
                 if j == 0:
 
                     @pl.when(k > 0)
                     def _():
-                        copy.wait_recv()
                         copy.wait_send()
                 else:
-                    copy.wait_recv()
                     copy.wait_send()
             if j > 0:
-                p_copy(k, j, block_of(k, 0)).wait_send()
+                p_copy(k, j, plane(k), b).wait_send()
 
     each(0, major, settle)
-    each(1, major, lambda k: z_copy(k, me).wait_send())
+    each(1, major, lambda k: z_copy(k, a).wait_send())
 
     def questions(k):
         copy = q_copy(k, lax.rem(me - k + n, n))
@@ -133,29 +177,33 @@
     each(1, n, questions)
 
 
-def gather(expander, asked, n, m):
+def gather(expander, asked, first, second, n, m):
     depth, width = expander.shape
+    rows, channels = first.shape
     dma = pltpu.SemaphoreType.DMA
     minor = minor_size(n)
+    major = n // minor
     vmem = pl.BlockSpec(memory_space=pltpu.VMEM)
+    embed = jax.ShapeDtypeStruct((rows, width), jnp.bfloat16)
     return pl.pallas_call(
         functools.partial(gather_kernel, n, m),
-        out_shape=(
-            jax.ShapeDtypeStruct((n, depth, width), expander.dtype),
-            jax.ShapeDtypeStruct(asked.shape, asked.dtype),
-        ),
-        in_specs=[vmem] * 2,
-        out_specs=(vmem, vmem),
+        out_shape=(jax.ShapeDtypeStruct(asked.shape, asked.dtype), embed, embed),
+        in_specs=[vmem] * 2 + [pl.BlockSpec(memory_space=pl.ANY)] * 2,
+        out_specs=(vmem,) * 3,
         scratch_shapes=[
-            dma((n // minor,)), dma((n // minor,)), dma((n,)), dma((n,)), dma((m * n,)), dma((m * n,)), dma((n,)), dma((n,)),
-        ],
+            pltpu.VMEM((major, minor * depth, width), expander.dtype),
+            pltpu.VMEM((2, rows, channels), first.dtype),
+            pltpu.VMEM((2, rows, width), jnp.float32),
+        ]
+        + [dma((size,)) for size in (major, n, m * n, n) for _ in range(2)]
+        + [dma((2,))],
         compiler_params=pltpu.CompilerParams(collective_id=0, has_side_effects=True, vmem_limit_bytes=40 << 20),
         name="gather",
-    )(expander, asked)
-
-
-def exchange_kernel(n, m, rows, gram, sums, got, out, total, landed, half, plane, line, last,
-                    s_core, s_all, rs, rr, os, orr, ps, pr, zs, zr, fs, fr, cs, cr, ss, sr):
+    )(expander, asked, first, second)
+
+
+def exchange_kernel(n, m, rows, gram, sums, got, out, s_all, landed, half, plane, line, last,
+                    s_core, rs, rr, os, orr, ps, pr, zs, zr, fs, fr, cs, cr, ss, sr):
     me, core = lax.axis_index("inner"), lax.axis_index("outer")
     minor = minor_size(n)
     major = n // minor
@@ -188,7 +236,7 @@
         return remote(line.at[other], last.at[k], (zs, zr), k, {"inner": other * minor + b})
 
     def s_copy(k, index):
-        return remote(s_all.at[index], s_all.at[index], (ss, sr), k, {"inner": lax.rem(me + k, n)})
+        return remote(s_core, s_all.at[index], (ss, sr), k, {"inner": lax.rem(me + k, n)})
 
     def f_copy(t, lanes):
         return remote(out.at[:, lanes], out.at[:, lanes], (fs, fr), t, {"outer": lax.rem(core + t, m)})
@@ -201,17 +249,20 @@
     s_core[core] = sums[...]
     for t in range(1, m):
         c_copy(t, lax.rem(core - t + m, m)).wait_recv()
-    s_all[me] = functools.reduce(lambda x, y: x + y, [s_core[t] for t in range(m)])
+    s_all[me] = s_core[...]
     each(1, n, lambda k: s_copy(k, me).start())
     for t in range(1, m):
         o_copy(t).wait_recv()
 
-    def add_cores(i):
-        x, y = i // minor, lax.rem(i, minor)
+    def over_cores(x, y):
         value = gram[x, y, :, mine]
         for t in range(1, m):
             value = value + landed[t, x, y]
-        half[x, y] = value
+        return value
+
+    def add_cores(i):
+        x, y = i // minor, lax.rem(i, minor)
+        half[x, y] = over_cores(x, y).astype(half.dtype)
 
     each(0, n, add_cores)
     for j in range(1, minor):
@@ -220,9 +271,9 @@
         p_copy(j).wait_recv()
 
     def add_plane(x):
-        value = half[x, b]
+        value = over_cores(x, b)
         for j in range(1, minor):
-            value = value + plane[j, x]
+            value = value + plane[j, x].astype(jnp.float32)
         line[x] = value
 
     each(0, major, add_plane)
@@ -235,10 +286,6 @@
     for t in range(1, m):
         f_copy(t, mine).start()
     each(1, n, lambda k: s_copy(k, lax.rem(me - k + n, n)).wait_recv())
-    value = s_all[0]
-    for k in range(1, n):
-        value = value + s_all[k]
-    total[...] = value
 
     def settle(k):
         r_copy(k, lax.rem(me - k + n, n)).wait_recv()
@@ -270,18 +317,17 @@
         out_shape=(
             jax.ShapeDtypeStruct(rows.shape, rows.dtype),
             jax.ShapeDtypeStruct((share, width), f32),
-            jax.ShapeDtypeStruct((1, width), f32),
+            jax.ShapeDtypeStruct((n, m, 1, width), f32),
         ),
         in_specs=[vmem] * 3,
         out_specs=(vmem,) * 3,
         scratch_shapes=[
             pltpu.VMEM((m, major, minor, share, part), f32),
-            pltpu.VMEM((major, minor, share, part), f32),
-            pltpu.VMEM((minor, major, share, part), f32),
+            pltpu.VMEM((major, minor, share, part), jnp.bfloat16),
+            pltpu.VMEM((minor, major, share, part), jnp.bfloat16),
             pltpu.VMEM((major, share, part), f32),
             pltpu.VMEM((major, share, part), f32),
             pltpu.VMEM((m, 1, width), f32),
-            pltpu.VMEM((n, 1, width), f32),
         ]
         + [dma((size,)) for size in pairs for _ in range(2)],
         compiler_params=pltpu.CompilerParams(collective_id=1, has_side_effects=True, vmem_limit_bytes=40 << 20),
@@ -309,11 +355,10 @@
     padded = -(-capacity // 128) * 128
     asked = jnp.sum(jnp.where(chosen, target_tile[:, None], 0), axis=0).reshape(group_size, 1, capacity)
     asked = jnp.pad(asked, ((0, 0), (0, 0), (0, padded - capacity)))
-    piece, wanted = gather(expander, asked, group_size, lax.axis_size("outer"))
-    piece = piece.reshape(-1, expand_width)
+    wanted, first_embed, second_embed = gather(
+        expander, asked, first_rows, second_rows, group_size, lax.axis_size("outer")
+    )
     wanted = wanted[:, 0, :capacity].reshape(slots)
-    first_embed = jnp.dot(first_rows, piece, preferred_element_type=jnp.float32).astype(jnp.bfloat16)
-    second_embed = jnp.dot(second_rows, piece, preferred_element_type=jnp.float32).astype(jnp.bfloat16)
     pick = (wanted[:, None] == row_index[None, :]).astype(jnp.bfloat16)
     send_rows = jnp.dot(pick, second_embed, preferred_element_type=jnp.float32).astype(jnp.bfloat16)
     counts = lax.dynamic_index_in_dim(tile_count, outer_pos, 0, keepdims=False)
@@ -321,15 +366,16 @@
     live = row_index < own_count
     masked = jnp.where(live[:, None], first_embed, jnp.zeros_like(first_embed))
     gram = lax.dot_general(masked, masked, (((0,), (0,)), ((), ())), preferred_element_type=jnp.float32)
-    recv_rows, gram_share, column_total = exchange(
+    sums = jnp.sum(masked.astype(jnp.float32), axis=0)
+    gram = gram - sums[:, None] * (sums / own_count.astype(jnp.float32))[None, :]
+    recv_rows, gram_share, all_sums = exchange(
         send_rows.reshape(group_size, capacity, expand_width),
         gram,
-        jnp.sum(masked.astype(jnp.float32), axis=0, keepdims=True),
+        sums[None, :],
         group_size,
         lax.axis_size("outer"),
     )
     recv_rows = recv_rows.reshape(slots, expand_width)
-    column_total = column_total[0]
     partner = jnp.dot(chosen.astype(jnp.bfloat16), recv_rows, preferred_element_type=jnp.float32)
     dest_count = jnp.sum(
         jnp.where(target_dev[:, None] == jnp.arange(group_size, dtype=jnp.int32)[None, :], counts[None, :], 0), axis=1
@@ -339,8 +385,15 @@
     invariance = jnp.where(valid, jnp.mean(diff * diff, axis=-1), jnp.float32(0.0))
     total = jnp.sum(tile_count).astype(jnp.float32)
     share_rows = expand_width // group_size
-    own_sums = lax.dynamic_slice_in_dim(column_total, inner_pos * share_rows, share_rows, 0)
-    covariance = (gram_share - own_sums[:, None] * column_total[None, :] / total) / (total - 1.0)
+    all_sums = all_sums.reshape(-1, expand_width)
+    column_total = jnp.sum(all_sums, axis=0)
+    own_part = lax.dynamic_slice_in_dim(all_sums, inner_pos * share_rows, share_rows, 1)
+    own_sums = jnp.sum(own_part, axis=0)
+    weights = 1.0 / tile_count.T.reshape(-1).astype(jnp.float32)
+    between = lax.dot_general(
+        own_part * weights[:, None], all_sums, (((0,), (0,)), ((), ())), precision=lax.Precision.HIGHEST
+    )
+    covariance = (gram_share + between - own_sums[:, None] * column_total[None, :] / total) / (total - 1.0)
     return (covariance, invariance[None, :])
 
 

time: 118 us -> 110 us (0.932); the launches traced: 118 us -> 109 us
  Pallas kernels: 94.6 us -> 88.1 us
  matrix products: 11.5 us -> 5.33 us
  local copies, waits for them, and re-layouts: 4.91 us -> 7.32 us
    pallas_call x1, Pallas kernels: 63.6 us -> 55.7 us  [exchange(): pl.pallas_call(functools.partial(exchange_kernel, n, m), out_shape=(jax.S...]
    dot_general x1, matrix products: 4.6 us -> 0.62 us  [shards(): jnp.dot(pick, second_embed, preferred_element_type=jnp.float32)]
    dot_general x1, matrix products: 3.88 us -> 1.21 us  [shards(): lax.dot_general(own_part * weights[:, None], all_sums, (((0,), (0,)), (()...]
    dot_general x1, matrix products: 0.75 us -> 2.78 us  [shards(): lax.dot_general(masked, masked, (((0,), (0,)), ((), ())), preferred_eleme...]
    unnamed x14, local copies, waits for them, and re-layouts: 4.04 us -> 5.59 us
    dot_general x1, matrix products: 2.23 us -> 0.72 us  [shards(): jnp.dot(chosen.astype(jnp.bfloat16), recv_rows, preferred_element_type=jn...]
    pallas_call x1, Pallas kernels: 31 us -> 32.4 us  [gather(): pl.pallas_call(functools.partial(gather_kernel, n, m), out_shape=(jax.Sha...]
where the time goes in v3:
time: 110 us; the launch traced here: 109 us
  Pallas kernels  88.1 us (80%)
  local copies, waits for them, and re-layouts  7.32 us (7%)
  other arithmetic  5.75 us (5%)
  matrix products  5.33 us (5%)
  between operations  2.07 us (2%)
    pallas_call x1, Pallas kernels, exchange(): pl.pallas_call(functools.partial(exchange_kernel, n, m), out_shape=(jax.S...  55.7 us
    pallas_call x1, Pallas kernels, gather(): pl.pallas_call(functools.partial(gather_kernel, n, m), out_shape=(jax.Sha...  32.4 us
    unnamed x14, local copies, waits for them, and re-layouts  5.59 us
    dot_general x1, matrix products, shards(): lax.dot_general(masked, masked, (((0,), (0,)), ((), ())), preferred_eleme...  2.78 us

profile of v3, /device:TPU:13, one launch (start us, length us, event | category | flops | bytes accessed | tf_op | source)
XLA Modules:
  0.0 108.6 jit_solution(2602967496169583189)
XLA Ops:
  0.6 1.3 %dynamic_slice.11 = s32[1,1]{1,0:T(1,128)} dynamic-slice(s32[2,16]{1,0:T(2,128)} %param.9, s32[]{:T(128)S(6)} %select_n.34, s32[]{:T(128)S(6)} %select_n.36), dynamic_slice_sizes={1,1} | dynamic-slice | bytes 12 | tf_op jit(solution)/shard_map/jit(dynamic_index_in_dim)/dynamic_slice | solution.py:365
  1.9 0.6 iota_compare_fusion.6
  2.6 0.9 convert_reduce_fusion.1
  3.5 0.7 multiply_add_fusion
  4.2 0.8 select_reduce_fusion
  5.0 0.1 reshape.70
  5.1 0.0 copy-start.1
  5.1 1.2 %copy-done.1 = bf16[1,256,2048]{2,1,0:T(8,128)(2,1)S(1)} copy-done((bf16[1,256,2048]{2,1,0:T(8,128)(2,1)S(1)}, bf16[1,256,2048]{2,1,0:T(8,128)(2,1)}, u32[]{:S(2)}) %copy-start.1) | copy-done | bytes 1048600
  6.4 0.0 copy-start.2
  6.4 1.2 %copy-done.2 = bf16[1,256,2048]{2,1,0:T(8,128)(2,1)S(1)} copy-done((bf16[1,256,2048]{2,1,0:T(8,128)(2,1)S(1)}, bf16[1,256,2048]{2,1,0:T(8,128)(2,1)}, u32[]{:S(2)}) %copy-start.2) | copy-done | bytes 1048600
  7.6 0.0 copy-start.3
  7.6 0.9 copy-done.3
  8.5 32.4 %gather.1 = (s32[16,1,128]{2,1,0:T(1,128)S(1)}, bf16[256,1024]{1,0:T(8,128)(2,1)S(1)}, bf16[256,1024]{1,0:T(8,128)(2,1)S(1)}) custom-call(bf16[128,1024]{1,0:T(8,128)(2,1)S(1)} %copy-done.3, s32[16,1,128]{2,1,0:T(1,128)S(1)} %pad.4.ask, bf16[256,2048]{1,0:T(8,128)(2,1)S(1)} %bitcast.20, bf16[256,2048]{1,0:T(8,128)(2,1)S(1)} %bitcast.21), custom_call_target="tpu_custom_call" | custom-call | tf_op jit(solution)/shard_map/gather/pallas_call | solution.py:188
  40.9 0.2 convert_reduce_fusion
  41.8 2.8 %multiply_subtract_fusion = f32[1024,1024]{1,0:T(8,128)} fusion(f32[1024]{0:T(1024)S(1)} %broadcast_divide_fusion, f32[1024]{0:T(1024)S(1)} %convert_reduce_fusion, bf16[256,1024]{1,0:T(8,128)(2,1)S(1)} %get-tuple-element.10, pred[256]{0:T(512)(128)(4,1)S(1)} %iota_compare_fusion.6), kind=kOutput, calls=%fused_computation | convolution fusion | flops 539230208 | bytes 4727040 | tf_op jit(solution)/shard_map/dot_general | solution.py:368
  44.6 0.1 eq.60
  44.7 0.6 convolution_convert_fusion
  45.3 0.0 copy-start
  45.3 2.2 %copy-done = f32[1024,1024]{1,0:T(8,128)S(1)} copy-done((f32[1024,1024]{1,0:T(8,128)S(1)}, f32[1024,1024]{1,0:T(8,128)}, u32[]{:S(2)}) %copy-start) | copy-done | bytes 4194328
  47.5 0.0 copy-start.5
  47.5 0.0 copy-start.4
  47.5 0.0 copy-start.6
  47.5 55.7 %exchange.1 = (bf16[16,48,1024]{2,1,0:T(8,128)(2,1)S(1)}, f32[64,1024]{1,0:T(8,128)S(1)}, f32[16,2,1,1024]{3,2,1,0:T(1,128)S(1)}) custom-call(bf16[16,48,1024]{2,1,0:T(8,128)(2,1)S(1)} %bitcast.19, f32[4,4,64,1024]{3,2,1,0:T(8,128)S(1)} %bitcast.18, f32[1,1024]{1,0:T(1,128)S(1)} %bitcast.22), custom_call_target="tpu_custom_call" | custom-call | tf_op jit(solution)/shard_map/exchange/pallas_call | solution.py:315
  103.2 0.7 fusion.1
  104.0 0.0 copy-done.5
  104.0 0.0 copy-done.4
  104.0 0.1 select_reduce_fusion.1
  104.1 0.0 copy-done.6
  104.1 1.2 %and_select_fusion = f32[1,256]{1,0:T(1,128)} fusion(f32[1,256]{1,0:T(1,128)S(1)} %bitcast.27, s32[1,256]{1,0:T(1,128)S(1)} %copy-done.6, s32[1,256]{1,0:T(1,128)S(1)} %bitcast.28, s32[]{:T(128)} %bitcast.5), kind=kLoop, calls=%fused_computation.25 | loop fusion | flops 1024 | bytes 4100 | tf_op jit(solution)/shard_map/jit(_where)/select_n | solution.py:385
  105.3 0.4 fusion.12
  105.7 0.1 reshape.73
  105.8 0.1 dynamic-slice_reduce_fusion
  105.9 0.6 reduce_sum.82
  107.2 0.1 copy.10
  107.3 0.1 div.51
  107.4 1.2 %fusion.3 = f32[64,1024]{1,0:T(8,128)} fusion(f32[64,1024]{1,0:T(8,128)S(1)} %get-tuple-element.11, f32[32,1024]{1,0:T(8,128)S(1)} %reshape.73, f32[]{:T(128)S(6)} %sub.14, f32[]{:T(128)S(6)} %convert_element_type.34, f32[1024]{0:T(1024)S(1)} %get-tuple-element.14, f32[64]{0:T(128)S(1)} %dynamic-slice_reduce_fusion, s32[]{:T(128)S(6)} %select_n.38, ...), kind=kOutput, calls=%fused_computation.7 | convolution fusion | flops 25495552 | bytes 676876 | tf_op jit(solution)/shard_map/dot_general | solution.py:393
  (6 shorter events, 0.1 us)
Async XLA Ops:
  5.1 1.2 %copy-start.1 = (bf16[1,256,2048]{2,1,0:T(8,128)(2,1)S(1)}, bf16[1,256,2048]{2,1,0:T(8,128)(2,1)}, u32[]{:S(2)}) copy-start(bf16[1,256,2048]{2,1,0:T(8,128)(2,1)} %param.6) | copy-start | bytes 3145732
  6.4 1.2 %copy-start.2 = (bf16[1,256,2048]{2,1,0:T(8,128)(2,1)S(1)}, bf16[1,256,2048]{2,1,0:T(8,128)(2,1)}, u32[]{:S(2)}) copy-start(bf16[1,256,2048]{2,1,0:T(8,128)(2,1)} %param.7) | copy-start | bytes 3145732
  7.6 0.9 copy-start.3
  45.3 2.2 %copy-start = (f32[1024,1024]{1,0:T(8,128)S(1)}, f32[1024,1024]{1,0:T(8,128)}, u32[]{:S(2)}) copy-start(f32[1024,1024]{1,0:T(8,128)} %multiply_subtract_fusion) | copy-start | bytes 12582916
  47.5 56.5 %copy-start.5 = (s32[2,16]{1,0:T(2,128)S(1)}, s32[2,16]{1,0:T(2,128)}, u32[]{:S(2)}) copy-start(s32[2,16]{1,0:T(2,128)} %param.9) | copy-start | bytes 388
  47.5 56.5 %copy-start.4 = (s32[1,256,1]{1,2,0:T(1,128)S(1)}, s32[1,256,1]{1,2,0:T(1,128)}, u32[]{:S(2)}) copy-start(s32[1,256,1]{1,2,0:T(1,128)} %param.10) | copy-start | bytes 3076
  47.5 56.6 %copy-start.6 = (s32[1,256]{1,0:T(1,128)S(1)}, s32[1,256]{1,0:T(1,128)}, u32[]{:S(2)}) copy-start(s32[1,256]{1,0:T(1,128)} %param.11) | copy-start | bytes 3076

commit v4 on v3

--- a/solution.py
+++ b/solution.py
@@ -47,8 +47,8 @@
     lax.fori_loop(low, high, step, 0)
 
 
-def gather_kernel(n, m, w, ask, first, second, got, first_embed, second_embed, full, feats, acc,
-                  zs, zr, ps, pr, os, orr, qs, qr, loads):
+def gather_part(n, m, w, ask, first, second, got, first_embed, second_embed, full, feats, acc,
+                zs, zr, ps, pr, os, orr, qs, qr, loads):
     me, core = lax.axis_index("inner"), lax.axis_index("outer")
     minor = minor_size(n)
     major = n // minor
@@ -177,33 +177,8 @@
     each(1, n, questions)
 
 
-def gather(expander, asked, first, second, n, m):
-    depth, width = expander.shape
-    rows, channels = first.shape
-    dma = pltpu.SemaphoreType.DMA
-    minor = minor_size(n)
-    major = n // minor
-    vmem = pl.BlockSpec(memory_space=pltpu.VMEM)
-    embed = jax.ShapeDtypeStruct((rows, width), jnp.bfloat16)
-    return pl.pallas_call(
-        functools.partial(gather_kernel, n, m),
-        out_shape=(jax.ShapeDtypeStruct(asked.shape, asked.dtype), embed, embed),
-        in_specs=[vmem] * 2 + [pl.BlockSpec(memory_space=pl.ANY)] * 2,
-        out_specs=(vmem,) * 3,
-        scratch_shapes=[
-            pltpu.VMEM((major, minor * depth, width), expander.dtype),
-            pltpu.VMEM((2, rows, channels), first.dtype),
-            pltpu.VMEM((2, rows, width), jnp.float32),
-        ]
-        + [dma((size,)) for size in (major, n, m * n, n) for _ in range(2)]
-        + [dma((2,))],
-        compiler_params=pltpu.CompilerParams(collective_id=0, has_side_effects=True, vmem_limit_bytes=40 << 20),
-        name="gather",
-    )(expander, asked, first, second)
-
-
-def exchange_kernel(n, m, rows, gram, sums, got, out, s_all, landed, half, plane, line, last,
-                    s_core, rs, rr, os, orr, ps, pr, zs, zr, fs, fr, cs, cr, ss, sr):
+def exchange_part(n, m, wanted, first_embed, second_embed, live, scale, got, out, s_all,
+                  masked, rows, gram, away, landed, half, plane, line, lined, last, sums, s_core, rs, rr, os, orr, ps, pr, zs, zr, fs, fr, cs, cr, ss, sr):
     me, core = lax.axis_index("inner"), lax.axis_index("outer")
     minor = minor_size(n)
     major = n // minor
@@ -214,11 +189,13 @@
         return pl.ds(pl.multiple_of(t * part, 128), part)
 
     mine = cols(core)
-    greet(n, m)
+    tiles, width = second_embed.shape
+    share, capacity = out.shape[0], rows.shape[1]
+    lanes = min(width, 256)
 
     def o_copy(t):
         peer = lax.rem(core + t, m)
-        return remote(gram.at[:, :, :, cols(peer)], landed.at[t], (os, orr), t, {"outer": peer})
+        return remote(away.at[:, cols(peer)], landed.at[t], (os, orr), t, {"outer": peer})
 
     def c_copy(t, index):
         return remote(sums, s_core.at[index], (cs, cr), t, {"outer": lax.rem(core + t, m)})
@@ -233,7 +210,7 @@
 
     def z_copy(k):
         other = lax.rem(a + k, major)
-        return remote(line.at[other], last.at[k], (zs, zr), k, {"inner": other * minor + b})
+        return remote(lined.at[other], last.at[k], (zs, zr), k, {"inner": other * minor + b})
 
     def s_copy(k, index):
         return remote(s_core, s_all.at[index], (ss, sr), k, {"inner": lax.rem(me + k, n)})
@@ -241,11 +218,42 @@
     def f_copy(t, lanes):
         return remote(out.at[:, lanes], out.at[:, lanes], (fs, fr), t, {"outer": lax.rem(core + t, m)})
 
+    def pick(j):
+        asked = wanted[j]
+        onehot = lax.broadcasted_iota(jnp.int32, (tiles, asked.shape[1]), 0) == asked
+        onehot = jnp.where(onehot, 1.0, 0.0).astype(jnp.bfloat16)
+        chosen = lax.dot_general(
+            onehot, second_embed[...], (((0,), (0,)), ((), ())), preferred_element_type=jnp.float32
+        )
+        rows[j] = chosen[:capacity].astype(rows.dtype)
+
+    def serve(i):
+        k = lax.rem(i + n // 2 - 1, n - 1) + 1
+        pick(lax.rem(me + k, n))
+        r_copy(k, me).start()
+
+    each(0, n - 1, serve)
+    pick(me)
+    got[me] = rows[me]
+    kept = first_embed[...].astype(jnp.float32) * live[...]
+    masked[...] = kept.astype(masked.dtype)
+    sums[...] = jnp.sum(kept, axis=0, keepdims=True)
     for t in range(1, m):
         c_copy(t, core).start()
+    ones = jnp.ones((tiles, 128), jnp.bfloat16)
+
+    def make_gram(c):
+        at = pl.ds(pl.multiple_of(c * lanes, lanes), lanes)
+        left = masked[:, at]
+        value = lax.dot_general(left, masked[...], (((0,), (0,)), ((), ())), preferred_element_type=jnp.float32)
+        column = lax.dot_general(left, ones, (((0,), (0,)), ((), ())), preferred_element_type=jnp.float32)
+        value = value - column[:, :1] * (sums[...] * scale[...])
+        gram[at, :] = value
+        away[at, :] = value.astype(away.dtype)
+
+    each(0, width // lanes, make_gram)
+    for t in range(1, m):
         o_copy(t).start()
-    each(1, n, lambda k: r_copy(k, me).start())
-    got[me] = rows[me]
     s_core[core] = sums[...]
     for t in range(1, m):
         c_copy(t, lax.rem(core - t + m, m)).wait_recv()
@@ -255,9 +263,10 @@
         o_copy(t).wait_recv()
 
     def over_cores(x, y):
-        value = gram[x, y, :, mine]
+        at = pl.ds(pl.multiple_of((x * minor + y) * share, share), share)
+        value = gram[at, mine]
         for t in range(1, m):
-            value = value + landed[t, x, y]
+            value = value + landed[t, at].astype(jnp.float32)
         return value
 
     def add_cores(i):
@@ -275,13 +284,14 @@
         for j in range(1, minor):
             value = value + plane[j, x].astype(jnp.float32)
         line[x] = value
+        lined[x] = value.astype(lined.dtype)
 
     each(0, major, add_plane)
     each(1, major, lambda k: z_copy(k).start())
     each(1, major, lambda k: z_copy(k).wait_recv())
     value = line[a]
     for k in range(1, major):
-        value = value + last[k]
+        value = value + last[k].astype(jnp.float32)
     out[:, mine] = value
     for t in range(1, m):
         f_copy(t, mine).start()
@@ -303,36 +313,58 @@
     each(1, major, lambda k: z_copy(k).wait_send())
 
 
-def exchange(rows, gram, sums, n, m):
-    width = gram.shape[1]
+def step_kernel(n, m, w, ask, first, second, live, scale, first_embed, got_rows, out, s_all, wanted, second_embed, *rest):
+    gather_part(n, m, w, ask, first, second, wanted, first_embed, second_embed, *rest[:12])
+    exchange_part(n, m, wanted, first_embed, second_embed, live, scale, got_rows, out, s_all, *rest[12:])
+
+
+def step(expander, asked, first, second, live, scale, capacity, n, m):
+    depth, width = expander.shape
+    rows, channels = first.shape
     share, part = width // n, width // m
     minor = minor_size(n)
     major = n // minor
     dma = pltpu.SemaphoreType.DMA
     vmem = pl.BlockSpec(memory_space=pltpu.VMEM)
-    f32 = jnp.float32
-    pairs = [n, m, minor, major, m, m, n]
+    anywhere = pl.BlockSpec(memory_space=pl.ANY)
+    bf16, f32 = jnp.bfloat16, jnp.float32
     return pl.pallas_call(
-        functools.partial(exchange_kernel, n, m),
+        functools.partial(step_kernel, n, m),
         out_shape=(
-            jax.ShapeDtypeStruct(rows.shape, rows.dtype),
+            jax.ShapeDtypeStruct((rows, width), bf16),
+            jax.ShapeDtypeStruct((n, capacity, width), bf16),
             jax.ShapeDtypeStruct((share, width), f32),
             jax.ShapeDtypeStruct((n, m, 1, width), f32),
         ),
-        in_specs=[vmem] * 3,
-        out_specs=(vmem,) * 3,
+        in_specs=[vmem, vmem, anywhere, anywhere, vmem, vmem],
+        out_specs=(vmem,) * 4,
         scratch_shapes=[
-            pltpu.VMEM((m, major, minor, share, part), f32),
-            pltpu.VMEM((major, minor, share, part), jnp.bfloat16),
-            pltpu.VMEM((minor, major, share, part), jnp.bfloat16),
+            pltpu.VMEM(asked.shape, asked.dtype),
+            pltpu.VMEM((rows, width), bf16),
+            pltpu.VMEM((major, minor * depth, width), bf16),
+            pltpu.VMEM((2, rows, channels), bf16),
+            pltpu.VMEM((2, rows, width), f32),
+        ]
+        + [dma((size,)) for size in (major, n, m * n, n) for _ in range(2)]
+        + [dma((2,))]
+        + [
+            pltpu.VMEM((rows, width), bf16),
+            pltpu.VMEM((n, capacity, width), bf16),
+            pltpu.VMEM((width, width), f32),
+            pltpu.VMEM((width, width), bf16),
+            pltpu.VMEM((m, width, part), bf16),
+            pltpu.VMEM((major, minor, share, part), bf16),
+            pltpu.VMEM((minor, major, share, part), bf16),
             pltpu.VMEM((major, share, part), f32),
-            pltpu.VMEM((major, share, part), f32),
+            pltpu.VMEM((major, share, part), bf16),
+            pltpu.VMEM((major, share, part), bf16),
+            pltpu.VMEM((1, width), f32),
             pltpu.VMEM((m, 1, width), f32),
         ]
-        + [dma((size,)) for size in pairs for _ in range(2)],
-        compiler_params=pltpu.CompilerParams(collective_id=1, has_side_effects=True, vmem_limit_bytes=40 << 20),
-        name="exchange",
-    )(rows, gram.reshape(major, minor, share, width), sums)
+        + [dma((size,)) for size in (n, m, minor, major, m, m, n) for _ in range(2)],
+        compiler_params=pltpu.CompilerParams(collective_id=0, has_side_effects=True, vmem_limit_bytes=48 << 20),
+        name="step",
+    )(expander, asked, first, second, live, scale)
 
 
 def shards(feats_first, feats_second, expander, tile_count, match_dev, match_tile):
@@ -355,23 +387,17 @@
     padded = -(-capacity // 128) * 128
     asked = jnp.sum(jnp.where(chosen, target_tile[:, None], 0), axis=0).reshape(group_size, 1, capacity)
     asked = jnp.pad(asked, ((0, 0), (0, 0), (0, padded - capacity)))
-    wanted, first_embed, second_embed = gather(
-        expander, asked, first_rows, second_rows, group_size, lax.axis_size("outer")
-    )
-    wanted = wanted[:, 0, :capacity].reshape(slots)
-    pick = (wanted[:, None] == row_index[None, :]).astype(jnp.bfloat16)
-    send_rows = jnp.dot(pick, second_embed, preferred_element_type=jnp.float32).astype(jnp.bfloat16)
     counts = lax.dynamic_index_in_dim(tile_count, outer_pos, 0, keepdims=False)
     own_count = lax.dynamic_index_in_dim(counts, inner_pos, 0, keepdims=False)
     live = row_index < own_count
-    masked = jnp.where(live[:, None], first_embed, jnp.zeros_like(first_embed))
-    gram = lax.dot_general(masked, masked, (((0,), (0,)), ((), ())), preferred_element_type=jnp.float32)
-    sums = jnp.sum(masked.astype(jnp.float32), axis=0)
-    gram = gram - sums[:, None] * (sums / own_count.astype(jnp.float32))[None, :]
-    recv_rows, gram_share, all_sums = exchange(
-        send_rows.reshape(group_size, capacity, expand_width),
-        gram,
-        sums[None, :],
+    first_embed, recv_rows, gram_share, all_sums = step(
+        expander,
+        asked,
+        first_rows,
+        second_rows,
+        live.astype(jnp.float32)[:, None],
+        jnp.full((1, expand_width), 1.0 / own_count.astype(jnp.float32)),
+        capacity,
         group_size,
         lax.axis_size("outer"),
     )

time: 110 us -> 95.5 us (0.87)
  Pallas kernels: 88.1 us -> 79.1 us
  matrix products: 5.33 us -> 1.96 us
  local copies, waits for them, and re-layouts: 7.32 us -> 5.05 us
    pallas_call x2 -> x1, Pallas kernels: 88.1 us -> 79.1 us  [step(): pl.pallas_call(functools.partial(step_kernel, n, m), out_shape=(jax.Shape...]
    dot_general x2 -> x0, matrix products: 3.4 us -> none  [the longest x1 2.78 us: shards(): lax.dot_general(masked, masked, (((0,), (0,)), ((), ())), preferred_eleme...]
    unnamed x14 -> x12, local copies, waits for them, and re-layouts: 5.59 us -> 3.41 us
where the time goes in v4:
time: 95.5 us; the launch traced here: 93.8 us
  Pallas kernels  79.1 us (83%)
  other arithmetic  5.57 us (6%)
  local copies, waits for them, and re-layouts  5.05 us (5%)
  between operations  2.1 us (2%)
  matrix products  1.96 us (2%)
    pallas_call x1, Pallas kernels, step(): pl.pallas_call(functools.partial(step_kernel, n, m), out_shape=(jax.Shape...  79.1 us
    unnamed x12, local copies, waits for them, and re-layouts  3.41 us

profile of v4, /device:TPU:13, one launch (start us, length us, event | category | flops | bytes accessed | tf_op | source)
XLA Modules:
  0.0 93.8 jit_solution(4746563718261053534)
XLA Ops:
  0.6 1.3 %dynamic_slice.11 = s32[1,1]{1,0:T(1,128)} dynamic-slice(s32[2,16]{1,0:T(2,128)} %param.9, s32[]{:T(128)S(6)} %select_n.30, s32[]{:T(128)S(6)} %select_n.32), dynamic_slice_sizes={1,1} | dynamic-slice | bytes 12 | tf_op jit(solution)/shard_map/jit(dynamic_index_in_dim)/dynamic_slice | solution.py:391
  1.9 0.7 fusion.6.live
  3.3 0.9 convert_reduce_fusion
  4.2 0.7 multiply_add_fusion
  4.9 0.8 select_reduce_fusion
  5.7 0.1 reshape.65
  5.8 0.0 copy-start
  5.8 1.2 %copy-done = bf16[1,256,2048]{2,1,0:T(8,128)(2,1)S(1)} copy-done((bf16[1,256,2048]{2,1,0:T(8,128)(2,1)S(1)}, bf16[1,256,2048]{2,1,0:T(8,128)(2,1)}, u32[]{:S(2)}) %copy-start) | copy-done | bytes 1048600
  7.1 0.0 copy-start.1
  7.1 1.2 %copy-done.1 = bf16[1,256,2048]{2,1,0:T(8,128)(2,1)S(1)} copy-done((bf16[1,256,2048]{2,1,0:T(8,128)(2,1)S(1)}, bf16[1,256,2048]{2,1,0:T(8,128)(2,1)}, u32[]{:S(2)}) %copy-start.1) | copy-done | bytes 1048600
  8.3 0.0 copy-start.2
  8.3 0.9 %copy-done.2 = bf16[128,1024]{1,0:T(8,128)(2,1)S(1)} copy-done((bf16[128,1024]{1,0:T(8,128)(2,1)S(1)}, bf16[128,1024]{1,0:T(8,128)(2,1)}, u32[]{:S(2)}) %copy-start.2) | copy-done | bytes 262168
  9.2 79.1 %step.1 = (bf16[256,1024]{1,0:T(8,128)(2,1)S(1)}, bf16[16,48,1024]{2,1,0:T(8,128)(2,1)S(1)}, f32[64,1024]{1,0:T(8,128)S(1)}, f32[16,2,1,1024]{3,2,1,0:T(1,128)S(1)}) custom-call(bf16[128,1024]{1,0:T(8,128)(2,1)S(1)} %copy-done.2, s32[16,1,128]{2,1,0:T(1,128)S(1)} %pad.4.ask, bf16[256,2048]{1,0:T(8,128)(2,1)S(1)} %bitcast.14, bf16[256,2048]{1,0:T(8,128)(2,1)S(1)} %bitcast.15, ...), custom_call_target="tpu_custom_call" | custom-call | tf_op jit(solution)/shard_map/step/pallas_call | solution.py:331
  88.3 0.0 copy-start.4
  88.3 0.0 copy-start.3
  88.4 0.0 copy-start.5
  88.4 0.7 fusion.1
  89.1 0.0 copy-done.4
  89.1 0.0 copy-done.3
  89.1 0.1 select_reduce_fusion.1
  89.2 0.0 copy-done.5
  89.2 1.2 %and_select_fusion = f32[1,256]{1,0:T(1,128)} fusion(f32[1,256]{1,0:T(1,128)S(1)} %bitcast.20, s32[1,256]{1,0:T(1,128)S(1)} %copy-done.5, s32[1,256]{1,0:T(1,128)S(1)} %bitcast.21, s32[]{:T(128)} %bitcast.4), kind=kLoop, calls=%fused_computation.20 | loop fusion | flops 1024 | bytes 4100 | tf_op jit(solution)/shard_map/jit(_where)/select_n | solution.py:411
  90.5 0.4 fusion.11
  90.9 0.1 reshape.66
  91.0 0.1 dynamic-slice_reduce_fusion
  91.1 0.6 reduce_sum.69
  92.4 0.1 copy.10
  92.5 0.1 div.43
  92.6 1.2 %fusion.3 = f32[64,1024]{1,0:T(8,128)} fusion(f32[64,1024]{1,0:T(8,128)S(1)} %get-tuple-element.6, f32[32,1024]{1,0:T(8,128)S(1)} %reshape.66, f32[]{:T(128)S(6)} %sub.10, f32[]{:T(128)S(6)} %convert_element_type.36, f32[1024]{0:T(1024)S(1)} %get-tuple-element.10, f32[64]{0:T(128)S(1)} %dynamic-slice_reduce_fusion, s32[]{:T(128)S(6)} %select_n.33, ...), kind=kOutput, calls=%fused_computation.5 | convolution fusion | flops 25495552 | bytes 676876 | tf_op jit(solution)/shard_map/dot_general | solution.py:419
  (5 shorter events, 0.0 us)
Async XLA Ops:
  5.8 1.2 %copy-start = (bf16[1,256,2048]{2,1,0:T(8,128)(2,1)S(1)}, bf16[1,256,2048]{2,1,0:T(8,128)(2,1)}, u32[]{:S(2)}) copy-start(bf16[1,256,2048]{2,1,0:T(8,128)(2,1)} %param.6) | copy-start | bytes 3145732
  7.1 1.2 %copy-start.1 = (bf16[1,256,2048]{2,1,0:T(8,128)(2,1)S(1)}, bf16[1,256,2048]{2,1,0:T(8,128)(2,1)}, u32[]{:S(2)}) copy-start(bf16[1,256,2048]{2,1,0:T(8,128)(2,1)} %param.7) | copy-start | bytes 3145732
  8.3 0.9 %copy-start.2 = (bf16[128,1024]{1,0:T(8,128)(2,1)S(1)}, bf16[128,1024]{1,0:T(8,128)(2,1)}, u32[]{:S(2)}) copy-start(bf16[128,1024]{1,0:T(8,128)(2,1)} %w.1) | copy-start | bytes 786436
  88.3 0.8 copy-start.4
  88.3 0.8 copy-start.3
  88.4 0.9 copy-start.5
